TPU v7x, 128 devices: a whole 4x4x4 slice. The times are simulated.
128 devices in a mesh: tm: 4 (over x), video: 32 (over y, z, core).
Axes of the slice: x: 4, y: 4, z: 4, core: 2. Of those that a mesh axis runs over, the one named last changes fastest.
Arguments:
- latent: bfloat16 [4, 3, 16, 12, 128, 16], P('tm', None, None, None, 'video'), may hold values from -6 to 6
- routing: int32 [16], replicated, may hold values from 0 to 15, each once
- counts: int32 [16], replicated, may hold values from 1 to 4, as said below
- offsets: int32 [16], replicated, may hold values from 0 to 3, as said below
- in_weight: bfloat16 [3, 3, 48, 384], replicated, may hold values from -0.3125 to 0.3125
- in_bias: float32 [384], replicated, may hold values from -3 to 3
- first_gain: float32 [384], replicated, may hold values from 0.1 to 1.9
- first_weight: bfloat16 [3, 3, 1152, 384], replicated, may hold values from -0.0625 to 0.0625
- first_bias: float32 [384], replicated, may hold values from -3 to 3
- second_gain: float32 [384], replicated, may hold values from 0.1 to 1.9
- second_weight: bfloat16 [3, 3, 1152, 384], replicated, may hold values from -0.0625 to 0.0625
- second_bias: float32 [384], replicated, may hold values from -3 to 3
Outputs:
- decoded: bfloat16 [4, 3, 192, 128, 384], P('tm', None, 'video')
Inputs may be any that keep to these rules, and one draw needn't show every extreme that they name: `routing`: a permutation: each video has its own decoder slot. `counts`: every video has at least one span. offsets[v] + counts[v] <= 4.
All inputs are finite; a program needn't handle non-finite values.
Results may differ from a plain program's by a relative error of at most 0.013.
Values may be sent and summed in bfloat16 or wider, within the bound.
No kernel may reach another device: no remote copies, remote signals or barrier semaphores. Data moves between devices by JAX's collectives and lax.ppermute only.
A program may use at most 384 MiB of HBM per device.

v0:
```python
import jax
import jax.numpy as jnp
from jax import lax
from jax.sharding import PartitionSpec as P

BANDS = 4
VPG = 2


def from_behind(value, axis, by):
    devices = lax.axis_size(axis)
    pairs = [(i, i + by) for i in range(devices) if 0 <= i + by < devices]
    return lax.ppermute(value, axis, pairs)


def padded_2(cells, sides, width):
    for axis, dim in sides:
        count = lax.axis_size(axis)
        head = lax.slice_in_dim(cells, 0, width, axis=dim)
        tail = lax.slice_in_dim(cells, cells.shape[dim] - width, cells.shape[dim], axis=dim)
        cells = jnp.concatenate(
            [
                lax.ppermute(tail, axis, [(i, (i + 1) % count) for i in range(count)]),
                cells,
                lax.ppermute(head, axis, [((i + 1) % count, i) for i in range(count)]),
            ],
            axis=dim,
        )
    return cells


def convolve(source, weight, bias_vec):
    frames = source.shape[1] - 2
    row_count = source.shape[2] - 2
    col_count = source.shape[3]
    padded = jnp.pad(source, ((0, 0), (0, 0), (0, 0), (1, 1), (0, 0)))
    summed = jnp.zeros(
        (source.shape[0], frames, row_count, col_count, weight.shape[-1]), jnp.float32
    )
    for step_t in range(3):
        for step_y in range(3):
            window = padded[:, step_t : step_t + frames, step_y : step_y + row_count]
            stacked = jnp.concatenate(
                [window[:, :, :, step_x : step_x + col_count] for step_x in range(3)], axis=-1
            )
            summed = summed + jnp.einsum(
                "pabcd,de->pabce",
                stacked,
                weight[step_t, step_y],
                preferred_element_type=jnp.float32,
            )
    return summed + bias_vec


def norm_silu(values, gain_vec):
    values = values.astype(jnp.float32)
    scaled = values * lax.rsqrt(jnp.mean(values * values, axis=-1, keepdims=True) + 1e-06)
    return jax.nn.silu(scaled * gain_vec).astype(jnp.bfloat16)


def row_keep(band_index, row_count, reach, window_rows):
    global_rows = band_index * row_count - reach + jnp.arange(row_count + 2 * reach)
    inside = (global_rows >= 0) & (global_rows < window_rows)
    return inside.astype(jnp.float32)[None, None, :, None, None]


def extend_time(frames_block):
    earlier = from_behind(frames_block[:, -2:], "tm", 1)
    return jnp.concatenate([earlier, frames_block], axis=1)


def on_device(
    latent,
    routing,
    counts,
    offsets,
    in_weight,
    in_bias,
    first_gain,
    first_weight,
    first_bias,
    second_gain,
    second_weight,
    second_bias,
):
    groups = lax.axis_size("video")
    group_count = groups // BANDS
    window_rows = latent.shape[3]
    row_count = window_rows // BANDS
    frames_per = latent.shape[1]
    local_cols = latent.shape[4]
    device_index = lax.axis_index("video")
    placed_index = (device_index + BANDS // 2) % groups
    group_index = placed_index // BANDS
    band_index = placed_index % BANDS
    span_index = lax.axis_index("tm")
    ordered = jnp.zeros_like(latent).at[:, :, routing].set(latent)
    outgoing = ordered.reshape(
        latent.shape[0], frames_per, group_count, VPG, BANDS, row_count, local_cols, latent.shape[5]
    )
    outgoing = jnp.transpose(outgoing, (0, 1, 2, 4, 3, 5, 6, 7))
    outgoing = outgoing.reshape(
        latent.shape[0], frames_per, groups, VPG, row_count, local_cols, latent.shape[5]
    )
    outgoing = jnp.roll(outgoing, -(BANDS // 2), axis=2)
    arrived = lax.all_to_all(outgoing, "video", split_axis=2, concat_axis=5, tiled=True)
    arrived = arrived.reshape(frames_per, VPG, row_count, -1, latent.shape[5])
    arrived = jnp.transpose(arrived, (1, 0, 2, 3, 4))
    slot_ids = group_index * VPG + jnp.arange(VPG, dtype=jnp.int32)
    chosen = routing[:, None] == slot_ids[None, :]
    first_span = jnp.sum(jnp.where(chosen, offsets[:, None], 0), axis=0)
    span_total = jnp.sum(jnp.where(chosen, counts[:, None], 0), axis=0)
    active = ((span_index >= first_span) & (span_index < first_span + span_total)).astype(
        jnp.float32
    )
    active = active[:, None, None, None, None]
    latent_frames = (arrived * active).astype(jnp.bfloat16)

    def frame_live(frame_count):
        relative = jnp.arange(frame_count, dtype=jnp.int32) - (frame_count - frames_per)
        span_of = span_index + jnp.floor_divide(relative, frames_per)
        inside = (span_of[None, :] >= first_span[:, None]) & (
            span_of[None, :] < (first_span + span_total)[:, None]
        )
        return inside.astype(jnp.float32)[:, :, None, None, None]

    def add_margins(frames_block):
        widened = padded_2(extend_time(frames_block), (("video", 2),), 1)
        return (widened * row_keep(band_index, row_count, 1, window_rows)).astype(jnp.bfloat16)

    hidden = convolve(add_margins(latent_frames), in_weight, in_bias)
    hidden = (hidden * frame_live(hidden.shape[1])).astype(jnp.bfloat16)
    middle = convolve(add_margins(norm_silu(hidden, first_gain)), first_weight, first_bias)
    middle = middle * frame_live(middle.shape[1])
    result = convolve(add_margins(norm_silu(middle, second_gain)), second_weight, second_bias)
    result = (result + hidden.astype(jnp.float32)) * active
    result = jnp.transpose(result.astype(jnp.bfloat16), (1, 0, 2, 3, 4))
    return result.reshape(frames_per, VPG * row_count, result.shape[3], result.shape[4])[None]


def solution(mesh):
    in_specs = (
        P("tm", None, None, None, "video", None),
        P(),
        P(),
        P(),
        P(),
        P(),
        P(),
        P(),
        P(),
        P(),
        P(),
        P(),
    )
    out_specs = P("tm", None, "video", None, None)
    return jax.shard_map(
        on_device, mesh=mesh, in_specs=in_specs, out_specs=out_specs, check_vma=False
    )
```

profile of v0, /device:TPU:2, one launch (start us, length us, event | category | flops | bytes accessed | tf_op | source)
XLA Modules:
  0.0 326.4 jit_solution(2240449142286560493)
XLA Ops:
  2.1 1.8 scatter_fusion
  6.7 8.3 %all-to-all-start = ((bf16[32,2,576]{2,1,0:T(2,128)(2,1)}), bf16[32,2,576]{2,1,0:T(2,128)(2,1)S(1)}, u32[]{:S(2)}, u32[]{:S(2)}) async-start(bf16[32,2,576]{2,1,0:T(2,128)(2,1)} %reshape.175), calls=%async_computation | async-start | bytes 163840 | tf_op jit(solution)/shard_map/all_to_all | solution.py:106
  15.3 7.3 %all-to-all-done = bf16[32,2,576]{2,1,0:T(2,128)(2,1)S(1)} async-done(((bf16[32,2,576]{2,1,0:T(2,128)(2,1)}), bf16[32,2,576]{2,1,0:T(2,128)(2,1)S(1)}, u32[]{:S(2)}, u32[]{:S(2)}) %all-to-all-start) | async-done | bytes 73760 | tf_op jit(solution)/shard_map/all_to_all | solution.py:106
  23.9 3.4 %collective-permute-start = (bf16[2,2,3,128,16]{3,4,2,1,0:T(8,128)(2,1)S(1)}, bf16[2,2,3,128,16]{3,4,2,1,0:T(8,128)(2,1)S(1)}, u32[]{:S(2)}, u32[]{:S(2)}) collective-permute-start(bf16[2,2,3,128,16]{3,4,2,1,0:T(8,128)(2,1)S(1)} %slice.615), channel_id=1, source_target_pairs={{0,32},{32,64},{64,96},{1,33},{33,65},{65,97},{2,34},{34,66},{66,9... | collective-permute-start | bytes 147464 | tf_op jit(solution)/shard_map/ppermute | solution.py:13
  27.4 2.5 collective-permute-done
  30.0 5.6 %collective-permute-start.2 = (bf16[2,5,1,128,16]{3,4,2,1,0:T(8,128)(2,1)S(1)}, bf16[2,5,1,128,16]{3,4,2,1,0:T(8,128)(2,1)S(1)}, u32[]{:S(2)}, u32[]{:S(2)}) collective-permute-start(bf16[2,5,1,128,16]{3,4,2,1,0:T(8,128)(2,1)S(1)} %get-tuple-element.95), channel_id=1, source_target_pairs={{1,0},{2,1},{3,2},{4,3},{5,4},{6,5},{7,6},{8,7},{9,8},{10,9},{11,1... | collective-permute-start | bytes 122888 | tf_op jit(solution)/shard_map/ppermute | solution.py:25
  39.2 1.4 fusion.165
  40.7 1.4 fusion.171
  42.1 1.4 fusion.177
  45.0 3.3 %fusion.189 = f32[2,3,3,128,384]{4,3,2,1,0:T(8,128)} fusion(bf16[2,3,3,128,16]{3,4,2,1,0:T(8,128)(2,1)S(1)} %get-tuple-element.78, bf16[2,3,3,128,16]{3,4,2,1,0:T(8,128)(2,1)S(1)} %get-tuple-element.88, bf16[2,3,3,128,16]{3,4,2,1,0:T(8,128)(2,1)S(1)} %get-tuple-element.77, bf16[3,3,48,384]{3,2,1,0:T(8,128)(2,1)} %param.16), kind=kOutput, calls=%fused_computation.222 | convolution fusion | flops 85598208 | bytes 3796992 | tf_op jit(solution)/shard_map/pabcd,de->pabce/dot_general | solution.py:46
  48.3 3.2 fusion.195
  51.5 3.2 fusion.201
  54.7 5.5 %fusion.108 = (f32[2,3,3,128]{3,2,1,0:T(4,128)S(1)}, f32[2,3,3,128,384]{4,3,2,1,0:T(8,128)S(1)}) fusion(f32[2,3]{1,0:T(2,128)S(1)} %and_convert_fusion.1, f32[384]{0:T(512)S(1)} %copy-done.25, bf16[3,3,48,384]{3,2,1,0:T(8,128)(2,1)} %param.16, bf16[2,3,3,128,16]{3,4,2,1,0:T(8,128)(2,1)S(1)} %get-tuple-element.83, ...), kind=kOutput, calls=%fused_computation.113 | convolution fusion | flops 97982208 | bytes 32119320 | tf_op jit(solution)/shard_map/pabcd,de->pabce/dot_general | solution.py:46
  61.9 3.4 %collective-permute-start.3 = (bf16[2,2,3,128,384]{4,3,2,1,0:T(8,128)(2,1)S(1)}, bf16[2,2,3,128,384]{4,3,2,1,0:T(8,128)(2,1)S(1)}, u32[]{:S(2)}, u32[]{:S(2)}) collective-permute-start(bf16[2,2,3,128,384]{4,3,2,1,0:T(8,128)(2,1)S(1)} %slice.625), channel_id=1, source_target_pairs={{0,32},{32,64},{64,96},{1,33},{33,65},{65,97},{2,34},{34,66},{66,9... | collective-permute-start | bytes 3538952 | tf_op jit(solution)/shard_map/ppermute | solution.py:13
  65.3 23.7 %collective-permute-done.3 = bf16[2,2,3,128,384]{4,3,2,1,0:T(8,128)(2,1)S(1)} collective-permute-done((bf16[2,2,3,128,384]{4,3,2,1,0:T(8,128)(2,1)S(1)}, bf16[2,2,3,128,384]{4,3,2,1,0:T(8,128)(2,1)S(1)}, u32[]{:S(2)}, u32[]{:S(2)}) %collective-permute-start.3) | collective-permute-done | bytes 1179680 | tf_op jit(solution)/shard_map/ppermute | solution.py:13
  89.3 5.2 %collective-permute-start.5 = (bf16[2,5,1,128,384]{4,3,2,1,0:T(8,128)(2,1)S(1)}, bf16[2,5,1,128,384]{4,3,2,1,0:T(8,128)(2,1)S(1)}, u32[]{:S(2)}, u32[]{:S(2)}) collective-permute-start(bf16[2,5,1,128,384]{4,3,2,1,0:T(8,128)(2,1)S(1)} %get-tuple-element.66), channel_id=1, source_target_pairs={{1,0},{2,1},{3,2},{4,3},{5,4},{6,5},{7,6},{8,7},{9,8},{10,9},{11,1... | collective-permute-start | bytes 2949128 | tf_op jit(solution)/shard_map/ppermute | solution.py:25
  94.5 11.6 %collective-permute-done.4 = bf16[2,5,1,128,384]{4,3,2,1,0:T(8,128)(2,1)S(1)} collective-permute-done((bf16[2,5,1,128,384]{4,3,2,1,0:T(8,128)(2,1)S(1)}, bf16[2,5,1,128,384]{4,3,2,1,0:T(8,128)(2,1)S(1)}, u32[]{:S(2)}, u32[]{:S(2)}) %collective-permute-start.4) | collective-permute-done | bytes 983072 | tf_op jit(solution)/shard_map/ppermute | solution.py:23
  106.1 1.5 multiply_convert_fusion.1
  107.7 4.2 %fusion.262 = (bf16[2,3,3,128,384]{4,3,2,1,0:T(8,128)(2,1)}, bf16[2,3,3,128,384]{4,3,2,1,0:T(8,128)(2,1)}, bf16[2,3,3,128,384]{4,3,2,1,0:T(8,128)(2,1)}, bf16[2,...) fusion(bf16[2,5,5,128,384]{4,3,2,1,0:T(8,128)(2,1)S(1)} %multiply_conve, ...), kind=kLoop, calls=%fused_computation.347 | loop fusion | bytes 24379392 | tf_op jit(solution)/shard_map/slice | solution.py:44
  111.9 11.0 %pad_slice_fusion.37 = (bf16[2,3,3,128,384]{4,3,2,1,0:T(8,128)(2,1)S(1)}, bf16[2,3,3,128,384]{4,3,2,1,0:T(8,128)(2,1)}, bf16[2,3,3,128,384]{4,3,2,1,0:T(8,128)(2...) fusion(bf16[2,5,5,128,384]{4,3,2,1,0:T(8,128)(2,1)S(1)} %multip, ...), kind=kLoop, calls=%fused_computation.329 | loop fusion | bytes 24379392 | tf_op jit(solution)/shard_map/slice | solution.py:44
  122.9 8.6 %pad_slice_fusion.36 = (bf16[2,3,3,128,384]{4,3,2,1,0:T(8,128)(2,1)S(1)}, bf16[2,3,3,128,384]{4,3,2,1,0:T(8,128)(2,1)}, bf16[2,3,3,128,384]{4,3,2,1,0:T(8,128)(2...) fusion(bf16[2,5,5,128,384]{4,3,2,1,0:T(8,128)(2,1)S(1)} %multip, ...), kind=kLoop, calls=%fused_computation.328 | loop fusion | bytes 29687808 | tf_op jit(solution)/shard_map/slice | solution.py:44
  131.5 7.8 %fusion = f32[2,3,3,128,384]{4,3,2,1,0:T(8,128)} fusion(bf16[2,3,3,128,384]{4,3,2,1,0:T(8,128)(2,1)} %get-tuple-element.37, bf16[2,3,3,128,384]{4,3,2,1,0:T(8,128)(2,1)} %get-tuple-element.61, bf16[2,3,3,128,384]{4,3,2,1,0:T(8,128)(2,1)} %get-tuple-element.62, bf16[3,3,1152,384]{3,2,1,0:T(8,128)(2,1)} %param.19), kind=kOutput, calls=%fused_computation.3 | convolution fusion | flops 2054356992 | bytes 9732096 | tf_op jit(solution)/shard_map/pabcd,de->pabce/dot_general | solution.py:46
  139.3 5.9 %fusion.6 = f32[2,3,3,128,384]{4,3,2,1,0:T(8,128)} fusion(bf16[2,3,3,128,384]{4,3,2,1,0:T(8,128)(2,1)S(1)} %copy-done.18, bf16[2,3,3,128,384]{4,3,2,1,0:T(8,128)(2,1)S(1)} %copy-done.8, bf16[2,3,3,128,384]{4,3,2,1,0:T(8,128)(2,1)S(1)} %copy-done.17, bf16[3,3,1152,384]{3,2,1,0:T(8,128)(2,1)} %param.19), kind=kOutput, calls=%fused_computation.9 | convolution fusion | flops 2054356992 | bytes 9732096 | tf_op jit(solution)/shard_map/pabcd,de->pabce/dot_general | solution.py:46
  145.3 6.8 %fusion.12 = f32[2,3,3,128,384]{4,3,2,1,0:T(8,128)} fusion(bf16[2,3,3,128,384]{4,3,2,1,0:T(8,128)(2,1)} %get-tuple-element.41, bf16[2,3,3,128,384]{4,3,2,1,0:T(8,128)(2,1)S(1)} %copy-done.5, bf16[2,3,3,128,384]{4,3,2,1,0:T(8,128)(2,1)S(1)} %copy-done.14, bf16[3,3,1152,384]{3,2,1,0:T(8,128)(2,1)} %param.19), kind=kOutput, calls=%fused_computation.15 | convolution fusion | flops 2054356992 | bytes 9732096 | tf_op jit(solution)/shard_map/pabcd,de->pabce/dot_general | solution.py:46
  152.2 5.8 %fusion.18 = f32[2,3,3,128,384]{4,3,2,1,0:T(8,128)} fusion(bf16[2,3,3,128,384]{4,3,2,1,0:T(8,128)(2,1)S(1)} %copy-done.11, bf16[2,3,3,128,384]{4,3,2,1,0:T(8,128)(2,1)S(1)} %copy-done.4, bf16[2,3,3,128,384]{4,3,2,1,0:T(8,128)(2,1)S(1)} %copy-done.10, bf16[3,3,1152,384]{3,2,1,0:T(8,128)(2,1)} %param.19), kind=kOutput, calls=%fused_computation.21 | convolution fusion | flops 2054356992 | bytes 9732096 | tf_op jit(solution)/shard_map/pabcd,de->pabce/dot_general | solution.py:46
  158.0 5.6 %fusion.24 = f32[2,3,3,128,384]{4,3,2,1,0:T(8,128)} fusion(bf16[2,3,3,128,384]{4,3,2,1,0:T(8,128)(2,1)S(1)} %copy-done.2, bf16[2,3,3,128,384]{4,3,2,1,0:T(8,128)(2,1)S(1)} %copy-done.3, bf16[2,3,3,128,384]{4,3,2,1,0:T(8,128)(2,1)S(1)} %copy-done.6, bf16[3,3,1152,384]{3,2,1,0:T(8,128)(2,1)} %param.19), kind=kOutput, calls=%fused_computation.27 | convolution fusion | flops 2054356992 | bytes 9732096 | tf_op jit(solution)/shard_map/pabcd,de->pabce/dot_general | solution.py:46
  163.6 5.6 %fusion.30 = f32[2,3,3,128,384]{4,3,2,1,0:T(8,128)} fusion(bf16[2,3,3,128,384]{4,3,2,1,0:T(8,128)(2,1)S(1)} %get-tuple-element.49, bf16[2,3,3,128,384]{4,3,2,1,0:T(8,128)(2,1)S(1)} %get-tuple-element.56, bf16[2,3,3,128,384]{4,3,2,1,0:T(8,128)(2,1)S(1)} %get-tuple-element.48, bf16[3,3,1152,384]{3,2,1,0:T(8,128)(2,1)} %param.19), kind=kOutput, calls=%fused_computation.33 | convolution fusion | flops 2054356992 | bytes 9732096 | tf_op jit(solution)/shard_map/pabcd,de->pabce/dot_general | solution.py:46
  169.3 5.6 %fusion.36 = f32[2,3,3,128,384]{4,3,2,1,0:T(8,128)} fusion(bf16[2,3,3,128,384]{4,3,2,1,0:T(8,128)(2,1)S(1)} %get-tuple-element.51, bf16[2,3,3,128,384]{4,3,2,1,0:T(8,128)(2,1)S(1)} %get-tuple-element.55, bf16[2,3,3,128,384]{4,3,2,1,0:T(8,128)(2,1)S(1)} %get-tuple-element.50, bf16[3,3,1152,384]{3,2,1,0:T(8,128)(2,1)} %param.19), kind=kOutput, calls=%fused_computation.39 | convolution fusion | flops 2054356992 | bytes 9732096 | tf_op jit(solution)/shard_map/pabcd,de->pabce/dot_general | solution.py:46
  174.9 5.6 %fusion.42 = f32[2,3,3,128,384]{4,3,2,1,0:T(8,128)} fusion(bf16[2,3,3,128,384]{4,3,2,1,0:T(8,128)(2,1)S(1)} %get-tuple-element.53, bf16[2,3,3,128,384]{4,3,2,1,0:T(8,128)(2,1)S(1)} %get-tuple-element.54, bf16[2,3,3,128,384]{4,3,2,1,0:T(8,128)(2,1)S(1)} %get-tuple-element.52, bf16[3,3,1152,384]{3,2,1,0:T(8,128)(2,1)} %param.19), kind=kOutput, calls=%fused_computation.45 | convolution fusion | flops 2054356992 | bytes 9732096 | tf_op jit(solution)/shard_map/pabcd,de->pabce/dot_general | solution.py:46
  180.5 11.8 %multiply_reduce_fusion = (f32[2,3,3,128]{3,2,1,0:T(4,128)S(1)}, f32[2,3,3,128,384]{4,3,2,1,0:T(8,128)S(1)}) fusion(f32[2,3]{1,0:T(2,128)S(1)} %and_convert_fusion.1, f32[384]{0:T(512)S(1)} %copy-done.21, bf16[3,3,1152,384]{3,2,1,0:T(8,128)(2,1)} %param.19, bf16[2,3,3,128,384]{4,3,2,1,0:T(8,128)(2,1)S(1)} %get-tuple-element.46, ...), kind=kOutput, calls=%fused_computation.127 | convolution fusion | flops 2064971520 | bytes 38054424 | tf_op jit(solution)/shard_map/pabcd,de->pabce/dot_general | solution.py:46
  192.4 1.5 multiply_convert_fusion.2
  194.0 3.4 %collective-permute-start.6 = (bf16[2,2,3,128,384]{4,3,2,1,0:T(8,128)(2,1)S(1)}, bf16[2,2,3,128,384]{4,3,2,1,0:T(8,128)(2,1)S(1)}, u32[]{:S(2)}, u32[]{:S(2)}) collective-permute-start(bf16[2,2,3,128,384]{4,3,2,1,0:T(8,128)(2,1)S(1)} %slice.635), channel_id=1, source_target_pairs={{0,32},{32,64},{64,96},{1,33},{33,65},{65,97},{2,34},{34,66},{66,9... | collective-permute-start | bytes 3538952 | tf_op jit(solution)/shard_map/ppermute | solution.py:13
  197.4 24.1 %collective-permute-done.6 = bf16[2,2,3,128,384]{4,3,2,1,0:T(8,128)(2,1)S(1)} collective-permute-done((bf16[2,2,3,128,384]{4,3,2,1,0:T(8,128)(2,1)S(1)}, bf16[2,2,3,128,384]{4,3,2,1,0:T(8,128)(2,1)S(1)}, u32[]{:S(2)}, u32[]{:S(2)}) %collective-permute-start.6) | collective-permute-done | bytes 1179680 | tf_op jit(solution)/shard_map/ppermute | solution.py:13
  221.8 5.1 %collective-permute-start.8 = (bf16[2,5,1,128,384]{4,3,2,1,0:T(8,128)(2,1)S(1)}, bf16[2,5,1,128,384]{4,3,2,1,0:T(8,128)(2,1)S(1)}, u32[]{:S(2)}, u32[]{:S(2)}) collective-permute-start(bf16[2,5,1,128,384]{4,3,2,1,0:T(8,128)(2,1)S(1)} %get-tuple-element.64), channel_id=1, source_target_pairs={{1,0},{2,1},{3,2},{4,3},{5,4},{6,5},{7,6},{8,7},{9,8},{10,9},{11,1... | collective-permute-start | bytes 2949128 | tf_op jit(solution)/shard_map/ppermute | solution.py:25
  226.9 11.7 %collective-permute-done.7 = bf16[2,5,1,128,384]{4,3,2,1,0:T(8,128)(2,1)S(1)} collective-permute-done((bf16[2,5,1,128,384]{4,3,2,1,0:T(8,128)(2,1)S(1)}, bf16[2,5,1,128,384]{4,3,2,1,0:T(8,128)(2,1)S(1)}, u32[]{:S(2)}, u32[]{:S(2)}) %collective-permute-start.7) | collective-permute-done | bytes 983072 | tf_op jit(solution)/shard_map/ppermute | solution.py:23
  238.6 1.5 multiply_convert_fusion
  240.2 3.2 fusion.261
  243.4 11.4 %pad_slice_fusion.19 = (bf16[2,3,3,128,384]{4,3,2,1,0:T(8,128)(2,1)}, bf16[2,3,3,128,384]{4,3,2,1,0:T(8,128)(2,1)}, bf16[2,3,3,128,384]{4,3,2,1,0:T(8,128)(2,1)}...) fusion(bf16[2,5,5,128,384]{4,3,2,1,0:T(8,128)(2,1)S(1)} %multip, ...), kind=kLoop, calls=%fused_computation.311 | loop fusion | bytes 24379392 | tf_op jit(solution)/shard_map/slice | solution.py:44
  254.8 8.7 %pad_slice_fusion.18 = (bf16[2,3,3,128,384]{4,3,2,1,0:T(8,128)(2,1)}, bf16[2,3,3,128,384]{4,3,2,1,0:T(8,128)(2,1)S(1)}, bf16[2,3,3,128,384]{4,3,2,1,0:T(8,128)(2...) fusion(bf16[2,5,5,128,384]{4,3,2,1,0:T(8,128)(2,1)S(1)} %multip, ...), kind=kLoop, calls=%fused_computation.310 | loop fusion | bytes 29687808 | tf_op jit(solution)/shard_map/slice | solution.py:44
  263.5 7.8 %fusion.54 = f32[2,3,3,128,384]{4,3,2,1,0:T(8,128)} fusion(bf16[2,3,3,128,384]{4,3,2,1,0:T(8,128)(2,1)} %get-tuple-element.10, bf16[2,3,3,128,384]{4,3,2,1,0:T(8,128)(2,1)} %get-tuple-element.34, bf16[2,3,3,128,384]{4,3,2,1,0:T(8,128)(2,1)} %get-tuple-element.35, bf16[3,3,1152,384]{3,2,1,0:T(8,128)(2,1)} %param.22), kind=kOutput, calls=%fused_computation.57 | convolution fusion | flops 2054356992 | bytes 9732096 | tf_op jit(solution)/shard_map/pabcd,de->pabce/dot_general | solution.py:46
  271.3 5.7 %fusion.60 = f32[2,3,3,128,384]{4,3,2,1,0:T(8,128)} fusion(bf16[2,3,3,128,384]{4,3,2,1,0:T(8,128)(2,1)S(1)} %copy-done.20, bf16[2,3,3,128,384]{4,3,2,1,0:T(8,128)(2,1)S(1)} %copy-done.9, bf16[2,3,3,128,384]{4,3,2,1,0:T(8,128)(2,1)S(1)} %copy-done.19, bf16[3,3,1152,384]{3,2,1,0:T(8,128)(2,1)} %param.22), kind=kOutput, calls=%fused_computation.63 | convolution fusion | flops 2054356992 | bytes 9732096 | tf_op jit(solution)/shard_map/pabcd,de->pabce/dot_general | solution.py:46
  277.1 5.9 %fusion.66 = f32[2,3,3,128,384]{4,3,2,1,0:T(8,128)} fusion(bf16[2,3,3,128,384]{4,3,2,1,0:T(8,128)(2,1)S(1)} %copy-done.16, bf16[2,3,3,128,384]{4,3,2,1,0:T(8,128)(2,1)S(1)} %get-tuple-element.33, bf16[2,3,3,128,384]{4,3,2,1,0:T(8,128)(2,1)S(1)} %copy-done.15, bf16[3,3,1152,384]{3,2,1,0:T(8,128)(2,1)} %param.22), kind=kOutput, calls=%fused_computation.69 | convolution fusion | flops 2054356992 | bytes 9732096 | tf_op jit(solution)/shard_map/pabcd,de->pabce/dot_general | solution.py:46
  282.9 5.9 %fusion.72 = f32[2,3,3,128,384]{4,3,2,1,0:T(8,128)} fusion(bf16[2,3,3,128,384]{4,3,2,1,0:T(8,128)(2,1)S(1)} %copy-done.13, bf16[2,3,3,128,384]{4,3,2,1,0:T(8,128)(2,1)S(1)} %get-tuple-element.32, bf16[2,3,3,128,384]{4,3,2,1,0:T(8,128)(2,1)S(1)} %copy-done.12, bf16[3,3,1152,384]{3,2,1,0:T(8,128)(2,1)} %param.22), kind=kOutput, calls=%fused_computation.75 | convolution fusion | flops 2054356992 | bytes 9732096 | tf_op jit(solution)/shard_map/pabcd,de->pabce/dot_general | solution.py:46
  288.9 5.6 %fusion.78 = f32[2,3,3,128,384]{4,3,2,1,0:T(8,128)} fusion(bf16[2,3,3,128,384]{4,3,2,1,0:T(8,128)(2,1)S(1)} %get-tuple-element.20, bf16[2,3,3,128,384]{4,3,2,1,0:T(8,128)(2,1)S(1)} %get-tuple-element.31, bf16[2,3,3,128,384]{4,3,2,1,0:T(8,128)(2,1)S(1)} %copy-done.7, bf16[3,3,1152,384]{3,2,1,0:T(8,128)(2,1)} %param.22), kind=kOutput, calls=%fused_computation.81 | convolution fusion | flops 2054356992 | bytes 9732096 | tf_op jit(solution)/shard_map/pabcd,de->pabce/dot_general | solution.py:46
  294.5 5.6 %fusion.84 = f32[2,3,3,128,384]{4,3,2,1,0:T(8,128)} fusion(bf16[2,3,3,128,384]{4,3,2,1,0:T(8,128)(2,1)S(1)} %get-tuple-element.22, bf16[2,3,3,128,384]{4,3,2,1,0:T(8,128)(2,1)S(1)} %get-tuple-element.29, bf16[2,3,3,128,384]{4,3,2,1,0:T(8,128)(2,1)S(1)} %get-tuple-element.21, bf16[3,3,1152,384]{3,2,1,0:T(8,128)(2,1)} %param.22), kind=kOutput, calls=%fused_computation.87 | convolution fusion | flops 2054356992 | bytes 9732096 | tf_op jit(solution)/shard_map/pabcd,de->pabce/dot_general | solution.py:46
  300.2 5.6 %fusion.90 = f32[2,3,3,128,384]{4,3,2,1,0:T(8,128)} fusion(bf16[2,3,3,128,384]{4,3,2,1,0:T(8,128)(2,1)S(1)} %get-tuple-element.24, bf16[2,3,3,128,384]{4,3,2,1,0:T(8,128)(2,1)S(1)} %get-tuple-element.28, bf16[2,3,3,128,384]{4,3,2,1,0:T(8,128)(2,1)S(1)} %get-tuple-element.23, bf16[3,3,1152,384]{3,2,1,0:T(8,128)(2,1)} %param.22), kind=kOutput, calls=%fused_computation.93 | convolution fusion | flops 2054356992 | bytes 9732096 | tf_op jit(solution)/shard_map/pabcd,de->pabce/dot_general | solution.py:46
  305.8 5.8 %fusion.96 = f32[2,3,3,128,384]{4,3,2,1,0:T(8,128)} fusion(bf16[2,3,3,128,384]{4,3,2,1,0:T(8,128)(2,1)S(1)} %get-tuple-element.26, bf16[2,3,3,128,384]{4,3,2,1,0:T(8,128)(2,1)S(1)} %get-tuple-element.27, bf16[2,3,3,128,384]{4,3,2,1,0:T(8,128)(2,1)S(1)} %get-tuple-element.25, bf16[3,3,1152,384]{3,2,1,0:T(8,128)(2,1)} %param.22), kind=kOutput, calls=%fused_computation.99 | convolution fusion | flops 2054356992 | bytes 9732096 | tf_op jit(solution)/shard_map/pabcd,de->pabce/dot_general | solution.py:46
  311.6 13.2 %fusion.118 = bf16[3,2,3,128,384]{4,3,2,0,1:T(8,128)(2,1)S(1)} fusion(f32[2,3,3,128,384]{4,3,2,1,0:T(8,128)} %fusion.96, f32[2,3,3,128,384]{4,3,2,1,0:T(8,128)} %fusion.90, f32[2,3,3,128,384]{4,3,2,1,0:T(8,128)} %fusion.84, f32[2,3,3,128,384]{4,3,2,1,0:T(8,128)} %fusion.78, f32[2,3,3,128,384]{4,3,2,1,0:T(8,128)} %fusion.72, ...), kind=kOutput, calls=%fused_computation.125 | convolution fusion | flops 2067628032 | bytes 39814688 | tf_op jit(solution)/shard_map/pabcd,de->pabce/dot_general | solution.py:46
  (106 shorter events, 15.6 us)
Async XLA Ops:
  3.9 11.2 %copy-start.28 = (s32[16]{0:T(128)S(1)}, s32[16]{0:T(128)}, u32[]{:S(2)}) copy-start(s32[16]{0:T(128)} %param.14) | copy-start | bytes 196
  3.9 11.2 %copy-start.29 = (s32[16]{0:T(128)S(1)}, s32[16]{0:T(128)}, u32[]{:S(2)}) copy-start(s32[16]{0:T(128)} %param.13) | copy-start | bytes 196
  3.9 11.2 %copy-start.30 = (s32[16]{0:T(128)S(1)}, s32[16]{0:T(128)}, u32[]{:S(2)}) copy-start(s32[16]{0:T(128)} %param.15) | copy-start | bytes 196
  6.7 15.9 %all-to-all-start = ((bf16[32,2,576]{2,1,0:T(2,128)(2,1)}), bf16[32,2,576]{2,1,0:T(2,128)(2,1)S(1)}, u32[]{:S(2)}, u32[]{:S(2)}) async-start(bf16[32,2,576]{2,1,0:T(2,128)(2,1)} %reshape.175), calls=%async_computation | async-start | bytes 163840 | tf_op jit(solution)/shard_map/all_to_all | solution.py:106
  15.3 22.0 %copy-start.23 = (f32[2]{0:T(128)}, f32[2]{0:T(128)S(1)}, u32[]{:S(2)}) copy-start(f32[2]{0:T(128)S(1)} %get-tuple-element.7) | copy-start | bytes 28
  23.9 6.0 %collective-permute-start = (bf16[2,2,3,128,16]{3,4,2,1,0:T(8,128)(2,1)S(1)}, bf16[2,2,3,128,16]{3,4,2,1,0:T(8,128)(2,1)S(1)}, u32[]{:S(2)}, u32[]{:S(2)}) collective-permute-start(bf16[2,2,3,128,16]{3,4,2,1,0:T(8,128)(2,1)S(1)} %slice.615), channel_id=1, source_target_pairs={{0,32},{32,64},{64,96},{1,33},{33,65},{65,97},{2,34},{34,66},{66,9... | collective-permute-start | bytes 147464 | tf_op jit(solution)/shard_map/ppermute | solution.py:13
  29.9 6.8 %collective-permute-start.1 = (bf16[2,5,1,128,16]{3,4,2,1,0:T(8,128)(2,1)S(1)}, bf16[2,5,1,128,16]{3,4,2,1,0:T(8,128)(2,1)S(1)}, u32[]{:S(2)}, u32[]{:S(2)}) collective-permute-start(bf16[2,5,1,128,16]{3,4,2,1,0:T(8,128)(2,1)S(1)} %get-tuple-element.94), channel_id=1, source_target_pairs={{0,1},{1,2},{2,3},{3,4},{4,5},{5,6},{6,7},{7,8},{8,9},{9,10},{10,1... | collective-permute-start | bytes 122888 | tf_op jit(solution)/shard_map/ppermute | solution.py:23
  30.0 7.2 %collective-permute-start.2 = (bf16[2,5,1,128,16]{3,4,2,1,0:T(8,128)(2,1)S(1)}, bf16[2,5,1,128,16]{3,4,2,1,0:T(8,128)(2,1)S(1)}, u32[]{:S(2)}, u32[]{:S(2)}) collective-permute-start(bf16[2,5,1,128,16]{3,4,2,1,0:T(8,128)(2,1)S(1)} %get-tuple-element.95), channel_id=1, source_target_pairs={{1,0},{2,1},{3,2},{4,3},{5,4},{6,5},{7,6},{8,7},{9,8},{10,9},{11,1... | collective-permute-start | bytes 122888 | tf_op jit(solution)/shard_map/ppermute | solution.py:25
  48.3 6.4 %copy-start.25 = (f32[384]{0:T(512)S(1)}, f32[384]{0:T(512)}, u32[]{:S(2)}) copy-start(f32[384]{0:T(512)} %param.17) | copy-start | bytes 4612
  54.6 5.5 %copy-start.26 = (f32[384]{0:T(512)S(1)}, f32[384]{0:T(512)}, u32[]{:S(2)}) copy-start(f32[384]{0:T(512)} %param.18) | copy-start | bytes 4612
  60.1 1.7 copy-start
  61.9 27.1 %collective-permute-start.3 = (bf16[2,2,3,128,384]{4,3,2,1,0:T(8,128)(2,1)S(1)}, bf16[2,2,3,128,384]{4,3,2,1,0:T(8,128)(2,1)S(1)}, u32[]{:S(2)}, u32[]{:S(2)}) collective-permute-start(bf16[2,2,3,128,384]{4,3,2,1,0:T(8,128)(2,1)S(1)} %slice.625), channel_id=1, source_target_pairs={{0,32},{32,64},{64,96},{1,33},{33,65},{65,97},{2,34},{34,66},{66,9... | collective-permute-start | bytes 3538952 | tf_op jit(solution)/shard_map/ppermute | solution.py:13
  89.2 16.9 %collective-permute-start.4 = (bf16[2,5,1,128,384]{4,3,2,1,0:T(8,128)(2,1)S(1)}, bf16[2,5,1,128,384]{4,3,2,1,0:T(8,128)(2,1)S(1)}, u32[]{:S(2)}, u32[]{:S(2)}) collective-permute-start(bf16[2,5,1,128,384]{4,3,2,1,0:T(8,128)(2,1)S(1)} %get-tuple-element.65), channel_id=1, source_target_pairs={{0,1},{1,2},{2,3},{3,4},{4,5},{5,6},{6,7},{7,8},{8,9},{9,10},{10,1... | collective-permute-start | bytes 2949128 | tf_op jit(solution)/shard_map/ppermute | solution.py:23
  89.3 16.8 %collective-permute-start.5 = (bf16[2,5,1,128,384]{4,3,2,1,0:T(8,128)(2,1)S(1)}, bf16[2,5,1,128,384]{4,3,2,1,0:T(8,128)(2,1)S(1)}, u32[]{:S(2)}, u32[]{:S(2)}) collective-permute-start(bf16[2,5,1,128,384]{4,3,2,1,0:T(8,128)(2,1)S(1)} %get-tuple-element.66), channel_id=1, source_target_pairs={{1,0},{2,1},{3,2},{4,3},{5,4},{6,5},{7,6},{8,7},{9,8},{10,9},{11,1... | collective-permute-start | bytes 2949128 | tf_op jit(solution)/shard_map/ppermute | solution.py:25
  131.5 7.8 %copy-start.8 = (bf16[2,3,3,128,384]{4,3,2,1,0:T(8,128)(2,1)S(1)}, bf16[2,3,3,128,384]{4,3,2,1,0:T(8,128)(2,1)}, u32[]{:S(2)}) copy-start(bf16[2,3,3,128,384]{4,3,2,1,0:T(8,128)(2,1)} %get-tuple-element.57) | copy-start | bytes 5308420
  131.5 7.8 %copy-start.17 = (bf16[2,3,3,128,384]{4,3,2,1,0:T(8,128)(2,1)S(1)}, bf16[2,3,3,128,384]{4,3,2,1,0:T(8,128)(2,1)}, u32[]{:S(2)}) copy-start(bf16[2,3,3,128,384]{4,3,2,1,0:T(8,128)(2,1)} %get-tuple-element.38) | copy-start | bytes 5308420
  131.5 7.8 %copy-start.18 = (bf16[2,3,3,128,384]{4,3,2,1,0:T(8,128)(2,1)S(1)}, bf16[2,3,3,128,384]{4,3,2,1,0:T(8,128)(2,1)}, u32[]{:S(2)}) copy-start(bf16[2,3,3,128,384]{4,3,2,1,0:T(8,128)(2,1)} %get-tuple-element.39) | copy-start | bytes 5308420
  139.3 6.0 %copy-start.5 = (bf16[2,3,3,128,384]{4,3,2,1,0:T(8,128)(2,1)S(1)}, bf16[2,3,3,128,384]{4,3,2,1,0:T(8,128)(2,1)}, u32[]{:S(2)}) copy-start(bf16[2,3,3,128,384]{4,3,2,1,0:T(8,128)(2,1)} %get-tuple-element.60) | copy-start | bytes 5308420
  139.3 6.0 %copy-start.14 = (bf16[2,3,3,128,384]{4,3,2,1,0:T(8,128)(2,1)S(1)}, bf16[2,3,3,128,384]{4,3,2,1,0:T(8,128)(2,1)}, u32[]{:S(2)}) copy-start(bf16[2,3,3,128,384]{4,3,2,1,0:T(8,128)(2,1)} %get-tuple-element.40) | copy-start | bytes 5308420
  145.3 6.9 %copy-start.4 = (bf16[2,3,3,128,384]{4,3,2,1,0:T(8,128)(2,1)S(1)}, bf16[2,3,3,128,384]{4,3,2,1,0:T(8,128)(2,1)}, u32[]{:S(2)}) copy-start(bf16[2,3,3,128,384]{4,3,2,1,0:T(8,128)(2,1)} %get-tuple-element.59) | copy-start | bytes 5308420
  145.3 6.9 %copy-start.10 = (bf16[2,3,3,128,384]{4,3,2,1,0:T(8,128)(2,1)S(1)}, bf16[2,3,3,128,384]{4,3,2,1,0:T(8,128)(2,1)}, u32[]{:S(2)}) copy-start(bf16[2,3,3,128,384]{4,3,2,1,0:T(8,128)(2,1)} %get-tuple-element.42) | copy-start | bytes 5308420
  145.3 6.8 %copy-start.11 = (bf16[2,3,3,128,384]{4,3,2,1,0:T(8,128)(2,1)S(1)}, bf16[2,3,3,128,384]{4,3,2,1,0:T(8,128)(2,1)}, u32[]{:S(2)}) copy-start(bf16[2,3,3,128,384]{4,3,2,1,0:T(8,128)(2,1)} %get-tuple-element.43) | copy-start | bytes 5308420
  152.1 5.8 %copy-start.2 = (bf16[2,3,3,128,384]{4,3,2,1,0:T(8,128)(2,1)S(1)}, bf16[2,3,3,128,384]{4,3,2,1,0:T(8,128)(2,1)}, u32[]{:S(2)}) copy-start(bf16[2,3,3,128,384]{4,3,2,1,0:T(8,128)(2,1)} %get-tuple-element.47) | copy-start | bytes 5308420
  152.2 5.8 %copy-start.3 = (bf16[2,3,3,128,384]{4,3,2,1,0:T(8,128)(2,1)S(1)}, bf16[2,3,3,128,384]{4,3,2,1,0:T(8,128)(2,1)}, u32[]{:S(2)}) copy-start(bf16[2,3,3,128,384]{4,3,2,1,0:T(8,128)(2,1)} %get-tuple-element.58) | copy-start | bytes 5308420
  152.2 5.8 %copy-start.6 = (bf16[2,3,3,128,384]{4,3,2,1,0:T(8,128)(2,1)S(1)}, bf16[2,3,3,128,384]{4,3,2,1,0:T(8,128)(2,1)}, u32[]{:S(2)}) copy-start(bf16[2,3,3,128,384]{4,3,2,1,0:T(8,128)(2,1)} %get-tuple-element.44) | copy-start | bytes 5308420
  174.9 5.6 %copy-start.21 = (f32[384]{0:T(512)S(1)}, f32[384]{0:T(512)}, u32[]{:S(2)}) copy-start(f32[384]{0:T(512)} %param.20) | copy-start | bytes 4612
  180.5 11.8 %copy-start.27 = (f32[384]{0:T(512)S(1)}, f32[384]{0:T(512)}, u32[]{:S(2)}) copy-start(f32[384]{0:T(512)} %param.21) | copy-start | bytes 4612
  194.0 27.5 %collective-permute-start.6 = (bf16[2,2,3,128,384]{4,3,2,1,0:T(8,128)(2,1)S(1)}, bf16[2,2,3,128,384]{4,3,2,1,0:T(8,128)(2,1)S(1)}, u32[]{:S(2)}, u32[]{:S(2)}) collective-permute-start(bf16[2,2,3,128,384]{4,3,2,1,0:T(8,128)(2,1)S(1)} %slice.635), channel_id=1, source_target_pairs={{0,32},{32,64},{64,96},{1,33},{33,65},{65,97},{2,34},{34,66},{66,9... | collective-permute-start | bytes 3538952 | tf_op jit(solution)/shard_map/ppermute | solution.py:13
  221.7 16.9 %collective-permute-start.7 = (bf16[2,5,1,128,384]{4,3,2,1,0:T(8,128)(2,1)S(1)}, bf16[2,5,1,128,384]{4,3,2,1,0:T(8,128)(2,1)S(1)}, u32[]{:S(2)}, u32[]{:S(2)}) collective-permute-start(bf16[2,5,1,128,384]{4,3,2,1,0:T(8,128)(2,1)S(1)} %get-tuple-element.63), channel_id=1, source_target_pairs={{0,1},{1,2},{2,3},{3,4},{4,5},{5,6},{6,7},{7,8},{8,9},{9,10},{10,1... | collective-permute-start | bytes 2949128 | tf_op jit(solution)/shard_map/ppermute | solution.py:23
  221.8 16.8 %collective-permute-start.8 = (bf16[2,5,1,128,384]{4,3,2,1,0:T(8,128)(2,1)S(1)}, bf16[2,5,1,128,384]{4,3,2,1,0:T(8,128)(2,1)S(1)}, u32[]{:S(2)}, u32[]{:S(2)}) collective-permute-start(bf16[2,5,1,128,384]{4,3,2,1,0:T(8,128)(2,1)S(1)} %get-tuple-element.64), channel_id=1, source_target_pairs={{1,0},{2,1},{3,2},{4,3},{5,4},{6,5},{7,6},{8,7},{9,8},{10,9},{11,1... | collective-permute-start | bytes 2949128 | tf_op jit(solution)/shard_map/ppermute | solution.py:25
  263.5 7.8 %copy-start.9 = (bf16[2,3,3,128,384]{4,3,2,1,0:T(8,128)(2,1)S(1)}, bf16[2,3,3,128,384]{4,3,2,1,0:T(8,128)(2,1)}, u32[]{:S(2)}) copy-start(bf16[2,3,3,128,384]{4,3,2,1,0:T(8,128)(2,1)} %get-tuple-element.30) | copy-start | bytes 5308420
  263.5 7.8 %copy-start.19 = (bf16[2,3,3,128,384]{4,3,2,1,0:T(8,128)(2,1)S(1)}, bf16[2,3,3,128,384]{4,3,2,1,0:T(8,128)(2,1)}, u32[]{:S(2)}) copy-start(bf16[2,3,3,128,384]{4,3,2,1,0:T(8,128)(2,1)} %get-tuple-element.11) | copy-start | bytes 5308420
  263.5 7.8 %copy-start.20 = (bf16[2,3,3,128,384]{4,3,2,1,0:T(8,128)(2,1)S(1)}, bf16[2,3,3,128,384]{4,3,2,1,0:T(8,128)(2,1)}, u32[]{:S(2)}) copy-start(bf16[2,3,3,128,384]{4,3,2,1,0:T(8,128)(2,1)} %get-tuple-element.12) | copy-start | bytes 5308420
  271.3 5.8 %copy-start.15 = (bf16[2,3,3,128,384]{4,3,2,1,0:T(8,128)(2,1)S(1)}, bf16[2,3,3,128,384]{4,3,2,1,0:T(8,128)(2,1)}, u32[]{:S(2)}) copy-start(bf16[2,3,3,128,384]{4,3,2,1,0:T(8,128)(2,1)} %get-tuple-element.13) | copy-start | bytes 5308420
  271.3 5.8 %copy-start.16 = (bf16[2,3,3,128,384]{4,3,2,1,0:T(8,128)(2,1)S(1)}, bf16[2,3,3,128,384]{4,3,2,1,0:T(8,128)(2,1)}, u32[]{:S(2)}) copy-start(bf16[2,3,3,128,384]{4,3,2,1,0:T(8,128)(2,1)} %get-tuple-element.14) | copy-start | bytes 5308420
  277.0 5.9 %copy-start.12 = (bf16[2,3,3,128,384]{4,3,2,1,0:T(8,128)(2,1)S(1)}, bf16[2,3,3,128,384]{4,3,2,1,0:T(8,128)(2,1)}, u32[]{:S(2)}) copy-start(bf16[2,3,3,128,384]{4,3,2,1,0:T(8,128)(2,1)} %get-tuple-element.15) | copy-start | bytes 5308420
  277.0 5.9 %copy-start.13 = (bf16[2,3,3,128,384]{4,3,2,1,0:T(8,128)(2,1)S(1)}, bf16[2,3,3,128,384]{4,3,2,1,0:T(8,128)(2,1)}, u32[]{:S(2)}) copy-start(bf16[2,3,3,128,384]{4,3,2,1,0:T(8,128)(2,1)} %get-tuple-element.16) | copy-start | bytes 5308420
  282.9 6.0 %copy-start.7 = (bf16[2,3,3,128,384]{4,3,2,1,0:T(8,128)(2,1)S(1)}, bf16[2,3,3,128,384]{4,3,2,1,0:T(8,128)(2,1)}, u32[]{:S(2)}) copy-start(bf16[2,3,3,128,384]{4,3,2,1,0:T(8,128)(2,1)} %get-tuple-element.17) | copy-start | bytes 5308420
  305.8 5.8 %copy-start.1 = (f32[2,3,3,128,384]{4,3,2,1,0:T(8,128)S(1)}, f32[2,3,3,128,384]{4,3,2,1,0:T(8,128)}, u32[]{:S(2)}) copy-start(f32[2,3,3,128,384]{4,3,2,1,0:T(8,128)} %copy-done) | copy-start | bytes 10616836
  305.8 5.8 %copy-start.22 = (f32[384]{0:T(512)S(1)}, f32[384]{0:T(512)}, u32[]{:S(2)}) copy-start(f32[384]{0:T(512)} %param.23) | copy-start | bytes 4612
  305.8 5.8 %copy-start.24 = (f32[2]{0:T(128)S(1)}, f32[2]{0:T(128)}, u32[]{:S(2)}) copy-start(f32[2]{0:T(128)} %copy-done.23) | copy-start | bytes 28
where the time goes:
time: 332 us; the launch traced here: 326 us
  matrix products  144 us (43%)
  waiting for transfers between devices  82.5 us (25%)
  local copies, waits for them, and re-layouts  56.5 us (17%)
  starting transfers between devices  34.6 us (10%)
  other arithmetic  7.82 us (2%)
    dot_general x27, matrix products, convolve(): jnp.einsum('pabcd,de->pabce', stacked, weight[step_t, step_y], preferred_...  144 us
    ppermute x3, waiting for transfers between devices, from_behind(): return lax.ppermute(value, axis, pairs)  50.3 us
    slice x8, local copies, waits for them, and re-layouts, convolve(): window[:, :, :, step_x:step_x + col_count]  47.6 us
    ppermute x3, waiting for transfers between devices, padded_2(): lax.ppermute(tail, axis, [(i, (i + 1) % count) for i in range(count)])  24.5 us
    ppermute x3, starting transfers between devices, padded_2(): lax.ppermute(head, axis, [((i + 1) % count, i) for i in range(count)])  15.8 us
    ppermute x3, starting transfers between devices, from_behind(): return lax.ppermute(value, axis, pairs)  10.2 us
    all_to_all x1, starting transfers between devices, on_device(): lax.all_to_all(outgoing, 'video', split_axis=2, concat_axis=5, tiled=True)  8.34 us
    all_to_all x1, waiting for transfers between devices, on_device(): lax.all_to_all(outgoing, 'video', split_axis=2, concat_axis=5, tiled=True)  7.27 us
  transfers between devices with their start and end apart: 10, of which 8 were waited for; matrix products, arithmetic and copies ran while one was open for 0% of the time, Pallas kernels for 0%

commit v1 on v0

v1 whole, which is shorter than its diff:
```python
import jax
import jax.numpy as jnp
import ml_dtypes
import numpy as np
from jax import lax
from jax.experimental import pallas as pl
from jax.experimental.pallas import tpu as pltpu
from jax.sharding import PartitionSpec as P

BANDS = 4
VPG = 2
F32 = jnp.float32
BF16 = jnp.bfloat16
VMEM_LIMIT = 60 << 20


def from_behind(value, axis, by):
    devices = lax.axis_size(axis)
    return lax.ppermute(value, axis, [(i, i + by) for i in range(devices - by)])


def neighbour_bands(value, axis, down):
    count = lax.axis_size(axis)
    pairs = []
    for device in range(count):
        band = ((device + BANDS // 2) % count) % BANDS
        if down and band < BANDS - 1:
            pairs.append((device, (device + 1) % count))
        if not down and band > 0:
            pairs.append((device, (device - 1) % count))
    return lax.ppermute(value, axis, pairs)


def act(values, gain):
    scale = lax.rsqrt(jnp.mean(values * values, axis=-1, keepdims=True) + 1e-06)
    half = values * scale * (0.5 * gain)
    return half * (1.0 + jnp.tanh(half))


def column_parts(even, odd):
    rows = even.shape[0]
    pair = lax.broadcasted_iota(jnp.int32, (rows, 1), 0) % 64
    odd_before = jnp.where(pair == 0, 0.0, pltpu.roll(odd, 1, 0))
    even_after = jnp.where(pair == 63, 0.0, pltpu.roll(even, rows - 1, 0))
    return odd_before - odd, even + odd, odd - even, even - even_after


def route_kernel(routing_ref, far_ref, near_ref, own_ref, sent_ref):
    rows = sent_ref.shape[0]
    lanes = own_ref.shape[0]
    slot_count = routing_ref.shape[0]
    lane = lax.broadcasted_iota(jnp.int32, (1, lanes), 1)
    slot_of_lane = jnp.full((1, lanes), -1, jnp.int32)
    for v in range(slot_count):
        slot_of_lane = jnp.where(lane // 4 == v, routing_ref[v], slot_of_lane)
    row = lax.broadcasted_iota(jnp.int32, (rows, 1), 0)
    placed = (row // 8 + BANDS // 2) % (rows // 8)
    slot_of_row = (placed // BANDS) * VPG + (row // 4) % VPG
    pick = (slot_of_row == slot_of_lane) & (row % 4 == lane % 4)
    pick = jnp.where(pick, 1.0, 0.0).astype(BF16)
    sent_ref[...] = jnp.zeros(sent_ref.shape, BF16)
    for s, ref in enumerate((far_ref, near_ref, own_ref)):
        moved = jnp.dot(pick, ref[...], preferred_element_type=F32)
        for pair in range(rows // 16):
            parts = []
            for device in (2 * pair, 2 * pair + 1):
                start = ((device + BANDS // 2) % BANDS) * 144
                parts.append(moved[device * 8 : device * 8 + 8, start : start + 336])
            block = jnp.concatenate(parts, axis=0).astype(BF16)
            sent_ref[pair * 16 : pair * 16 + 16, s * 384 : s * 384 + 336] = block


def weight_kernel(taps_ref, out_ref):
    depth = out_ref.shape[2]
    g0, g1, g2 = (taps_ref[0, k * depth : (k + 1) * depth, :] for k in range(3))
    ends = 0.5 * (g0.astype(F32) + g2.astype(F32))
    middle = 0.5 * g1.astype(F32)
    out_ref[0, 0] = g0
    out_ref[1, 0] = (ends + middle).astype(BF16)
    out_ref[2, 0] = (ends - middle).astype(BF16)
    out_ref[3, 0] = g2


def column_weights(weight):
    a, b, depth, channels = weight.shape
    taps = weight.reshape(a * b, depth, channels)
    shape = (4, a * b, depth // 3, channels)
    return pl.pallas_call(
        weight_kernel,
        grid=(a * b,),
        in_specs=[pl.BlockSpec((1, depth, channels), lambda t: (t, 0, 0))],
        out_specs=pl.BlockSpec((4, 1, depth // 3, channels), lambda t: (0, t, 0, 0)),
        out_shape=jax.ShapeDtypeStruct(shape, BF16),
        compiler_params=pltpu.CompilerParams(vmem_limit_bytes=16 << 20),
        cost_estimate=pl.CostEstimate(
            flops=0, bytes_accessed=2 * weight.size + 8 * weight.size // 3, transcendentals=0
        ),
        name="column_weights",
    )(taps)


def video_spans(place_ref, routing_ref, counts_ref, offsets_ref):
    found = []
    for p in range(VPG):
        slot = (place_ref[0] // BANDS) * VPG + p
        first = jnp.int32(0)
        end = jnp.int32(0)
        for v in range(routing_ref.shape[0]):
            here = routing_ref[v] == slot
            first = jnp.where(here, offsets_ref[v], first)
            end = jnp.where(here, offsets_ref[v] + counts_ref[v], end)
        found.append((first, end))
    return found


def live_mask(spans, span, inside, rows):
    flags = [
        jnp.where((span >= first) & (span < end) & inside, 1.0, 0.0) for first, end in spans
    ]
    row = lax.broadcasted_iota(jnp.int32, (rows, 1), 0)
    return jnp.where(row < rows // 2, flags[0], flags[1])


def input_kernel(
    place_ref,
    routing_ref,
    counts_ref,
    offsets_ref,
    planes_ref,
    weight_ref,
    bias_ref,
    gain_ref,
    parts_ref,
    hidden_ref,
):
    row = pl.program_id(0)
    frames = parts_ref.shape[2] // 128
    bias = bias_ref[...]
    gain = gain_ref[...]
    spans = video_spans(place_ref, routing_ref, counts_ref, offsets_ref)
    window_row = (place_ref[0] % BANDS) * 3 - 1 + row
    inside = (window_row >= 0) & (window_row < 3 * BANDS)
    for f in range(frames):
        taps = []
        for a in range(3):
            for b in range(3):
                s, k = divmod(f + a, 3)
                start = pl.multiple_of(s * 384 + k * 16 + (row + b) * 48, 16)
                tap = planes_ref[pl.ds(start, 16), :]
                taps += [tap[:, p * 128 : (p + 1) * 128] for p in range(4)]
        patch = jnp.concatenate(taps, axis=0)
        both = lax.dot_general(
            patch, weight_ref[...], (((0,), (0,)), ((), ())), preferred_element_type=F32
        )
        span = place_ref[1] + (f + 2) // 3 - 2
        mask = live_mask(spans, span, inside, 128)
        sides = []
        for side in range(2):
            values = both[:, side * 384 : (side + 1) * 384] + bias
            hidden = (values * mask).astype(BF16)
            if f >= frames - 3:

                @pl.when(row < 4)
                def _(hidden=hidden, f=f, side=side):
                    hidden_ref[0, f - (frames - 3), side] = hidden

            sides.append(act(hidden.astype(F32), gain))
        for i, part in enumerate(column_parts(*sides)):
            parts_ref[i, 0, f * 128 : (f + 1) * 128, :] = part.astype(BF16)


def products(load, weight_ref, rows, size):
    total = None
    for b in range(3):
        for a in range(3):
            term = jnp.dot(
                load(rows + b, a * 128, size), weight_ref[0, 3 * a + b], preferred_element_type=F32
            )
            total = term if total is None else total + term
    return total


def first_kernel(
    place_ref,
    routing_ref,
    counts_ref,
    offsets_ref,
    parts_ref,
    weight_ref,
    bias_ref,
    gain_ref,
    top_ref,
    bottom_ref,
    second_ref,
    terms_ref,
):
    step = pl.program_id(0)
    out_rows = terms_ref.shape[1]
    size = terms_ref.shape[2]
    for row in range(out_rows):
        terms_ref[step, row] = products(
            lambda r, start, n: parts_ref[0, r, start : start + n, :], weight_ref, row, size
        )

    @pl.when(step == 3)
    def _():
        bias = bias_ref[...]
        gain = gain_ref[...]
        spans = video_spans(place_ref, routing_ref, counts_ref, offsets_ref)
        for row in range(out_rows):

            def one_frame(f, carry):
                at = pl.ds(pl.multiple_of(f * 128, 128), 128)
                span = place_ref[1] + (f + 1) // 3 - 1
                mask = live_mask(spans, span, True, 128)
                mixed = terms_ref[1, row, at], terms_ref[2, row, at]
                even = terms_ref[0, row, at] + mixed[0] + mixed[1]
                odd = mixed[0] - mixed[1] - terms_ref[3, row, at]
                even = act((even + bias) * mask, gain)
                odd = act((odd + bias) * mask, gain)
                for edge_row, ref in ((0, top_ref), (out_rows - 1, bottom_ref)):
                    if row == edge_row:
                        ref[f, 0] = even.astype(BF16)
                        ref[f, 1] = odd.astype(BF16)
                for i, part in enumerate(column_parts(even, odd)):
                    second_ref[i, row, at, :] = part.astype(BF16)
                return carry

            lax.fori_loop(0, size // 128, one_frame, 0)


def second_kernel(
    place_ref,
    routing_ref,
    counts_ref,
    offsets_ref,
    parts_ref,
    above_ref,
    below_ref,
    weight_ref,
    bias_ref,
    hidden_ref,
    out_ref,
    halo_ref,
    terms_ref,
    line_ref,
):
    step = pl.program_id(0)
    out_rows = terms_ref.shape[1]
    size = terms_ref.shape[2]

    @pl.when(step == 0)
    def _():
        def one_frame(f, carry):
            at = pl.ds(pl.multiple_of(f * 128, 128), 128)
            for side, ref in enumerate((above_ref, below_ref)):
                even, odd = ref[f, 0].astype(F32), ref[f, 1].astype(F32)
                for i, part in enumerate(column_parts(even, odd)):
                    halo_ref[i, side, at, :] = part.astype(BF16)
            return carry

        lax.fori_loop(0, halo_ref.shape[2] // 128, one_frame, 0)

    def load(row, start, n):
        if row == 0:
            return halo_ref[step, 0, start : start + n, :]
        if row == out_rows + 1:
            return halo_ref[step, 1, start : start + n, :]
        return parts_ref[0, row - 1, start : start + n, :]

    for row in range(out_rows):
        terms_ref[step, row] = products(load, weight_ref, row, size)

    @pl.when(step == 3)
    def _():
        bias = bias_ref[...]
        spans = video_spans(place_ref, routing_ref, counts_ref, offsets_ref)
        lives = [
            jnp.where((place_ref[1] >= first) & (place_ref[1] < end), 1.0, 0.0)
            for first, end in spans
        ]
        for row in range(out_rows):

            def one_frame(f, carry):
                for video in range(2):
                    at = pl.ds(pl.multiple_of(f * 128 + video * 64, 64), 64)
                    mixed = terms_ref[1, row, at], terms_ref[2, row, at]
                    even = terms_ref[0, row, at] + mixed[0] + mixed[1]
                    odd = mixed[0] - mixed[1] - terms_ref[3, row, at]
                    here = slice(video * 64, video * 64 + 64)
                    live = lives[video]
                    even = (even + bias + hidden_ref[row, f, 0, here].astype(F32)) * live
                    odd = (odd + bias + hidden_ref[row, f, 1, here].astype(F32)) * live
                    for lane in range(3):
                        cut = slice(lane * 128, lane * 128 + 128)
                        line_ref[lane, pl.ds(0, 64, stride=2), :] = even[:, cut]
                        line_ref[lane, pl.ds(1, 64, stride=2), :] = odd[:, cut]
                    for lane in range(3):
                        cut = slice(lane * 128, lane * 128 + 128)
                        out_ref[f, video * out_rows + row, :, cut] = line_ref[lane].astype(BF16)
                return carry

            lax.fori_loop(0, size // 128, one_frame, 0)


def whole(shape):
    return pl.BlockSpec(shape, lambda *_: (0,) * len(shape))


def by_step(shape):
    return pl.BlockSpec(shape, lambda i: (i,) + (0,) * (len(shape) - 1))


SMEM = pl.BlockSpec(memory_space=pltpu.SMEM)
VMEM = pl.BlockSpec(memory_space=pltpu.VMEM)


def params():
    return pltpu.CompilerParams(vmem_limit_bytes=VMEM_LIMIT)


def on_device(
    latent,
    routing,
    counts,
    offsets,
    in_weight,
    in_bias,
    first_gain,
    first_weight,
    first_bias,
    second_gain,
    second_weight,
    second_bias,
):
    groups = lax.axis_size("video")
    spans = lax.axis_size("tm")
    _, span_frames, videos, window_rows, local_cols, zdim = latent.shape
    row_count = window_rows // BANDS
    channels = in_weight.shape[-1]
    pairs = groups * local_cols // 2
    span_index = lax.axis_index("tm")
    device_index = lax.axis_index("video")

    live = (span_index >= offsets) & (span_index < offsets + counts)
    own = jnp.transpose(latent[0], (1, 3, 2, 0, 4)) * live[:, None, None, None, None].astype(BF16)
    own = jnp.pad(own, ((0, 0), (0, 0), (2, 2), (0, 0), (0, 0)))
    own = own.reshape(videos * local_cols, (window_rows + 4) * span_frames * zdim)
    near, far = from_behind(own, "tm", 1), from_behind(own, "tm", 2)
    frames = 3 * span_frames
    sent = pl.pallas_call(
        route_kernel,
        in_specs=[SMEM] + [VMEM] * 3,
        out_specs=VMEM,
        out_shape=jax.ShapeDtypeStruct((groups * VPG * local_cols, 3 * 384), BF16),
        compiler_params=pltpu.CompilerParams(vmem_limit_bytes=16 << 20),
        name="route",
    )(routing, far, near, own)
    sent = sent.reshape(groups, VPG * local_cols, 3 * 384)
    got = lax.all_to_all(sent, "video", 0, 0, tiled=True)

    source = np.arange(groups * VPG * local_cols)
    source_col = (source // (VPG * local_cols)) * local_cols + source % local_cols
    source_video = (source // local_cols) % VPG
    pair = np.arange(pairs)
    wanted = np.stack([2 * pair - 1, 2 * pair, 2 * pair + 1, 2 * pair + 2])
    lanes = (source_col[:, None, None, None] == wanted[:, None, :]) & (
        source_video[:, None, None, None] == np.arange(VPG)[:, None]
    )
    lanes = lanes.reshape(source.size, 4 * VPG * pairs).astype(ml_dtypes.bfloat16)
    planes = lax.dot_general(
        got.reshape(source.size, 3 * 384),
        lanes,
        (((0,), (0,)), ((), ())),
        preferred_element_type=F32,
    ).astype(BF16)
    my_placed = (device_index + BANDS // 2) % groups
    place = jnp.stack([my_placed, span_index])
    scalars = (place, routing, counts, offsets)

    in_frames, mid_frames = frames - 2, frames - 4
    width = VPG * pairs
    rows5_n = row_count + 2

    zero = jnp.zeros(in_weight.shape[:2] + (zdim, channels), BF16)
    in_taps = jnp.concatenate(
        [
            jnp.concatenate([in_weight, zero], axis=2),
            jnp.concatenate([zero, in_weight], axis=2),
        ],
        axis=3,
    ).reshape(-1, 2 * channels)

    first_parts, hidden = pl.pallas_call(
        input_kernel,
        grid=(rows5_n,),
        in_specs=[
            *[SMEM] * 4,
            whole(planes.shape),
            whole(in_taps.shape),
            whole((channels,)),
            whole((channels,)),
        ],
        out_specs=[
            pl.BlockSpec((4, 1, in_frames * width, channels), lambda r: (0, r, 0, 0)),
            pl.BlockSpec(
                (1, span_frames, 2, width, channels),
                lambda r: (jnp.clip(r - 1, 0, row_count - 1), 0, 0, 0, 0),
            ),
        ],
        out_shape=[
            jax.ShapeDtypeStruct((4, rows5_n, in_frames * width, channels), BF16),
            jax.ShapeDtypeStruct((row_count, span_frames, 2, width, channels), BF16),
        ],
        compiler_params=params(),
        name="input_conv",
    )(*scalars, planes, in_taps, in_bias, first_gain)

    top, bottom, second_parts = pl.pallas_call(
        first_kernel,
        grid=(4,),
        in_specs=[
            *[SMEM] * 4,
            by_step((1, rows5_n, in_frames * width, channels)),
            by_step((1, 9, channels, channels)),
            whole((channels,)),
            whole((channels,)),
        ],
        out_specs=[
            whole((mid_frames, 2, width, channels)),
            whole((mid_frames, 2, width, channels)),
            whole((4, row_count, mid_frames * width, channels)),
        ],
        out_shape=[
            jax.ShapeDtypeStruct((mid_frames, 2, width, channels), BF16),
            jax.ShapeDtypeStruct((mid_frames, 2, width, channels), BF16),
            jax.ShapeDtypeStruct((4, row_count, mid_frames * width, channels), BF16),
        ],
        scratch_shapes=[pltpu.VMEM((4, row_count, mid_frames * width, channels), F32)],
        compiler_params=params(),
        name="first_conv",
    )(*scalars, first_parts, column_weights(first_weight), first_bias, second_gain)

    above = neighbour_bands(bottom, "video", True)
    below = neighbour_bands(top, "video", False)

    out = pl.pallas_call(
        second_kernel,
        grid=(4,),
        in_specs=[
            *[SMEM] * 4,
            by_step((1, row_count, mid_frames * width, channels)),
            whole(above.shape),
            whole(below.shape),
            by_step((1, 9, channels, channels)),
            whole((channels,)),
            pl.BlockSpec((row_count, span_frames, 2, width, channels), lambda i: (0, 0, 0, 0, 0)),
        ],
        out_specs=whole((span_frames, VPG * row_count, 2 * pairs, channels)),
        out_shape=jax.ShapeDtypeStruct((span_frames, VPG * row_count, 2 * pairs, channels), BF16),
        scratch_shapes=[
            pltpu.VMEM((4, 2, mid_frames * width, channels), BF16),
            pltpu.VMEM((4, row_count, span_frames * width, channels), F32),
            pltpu.VMEM((3, 2 * pairs, 128), F32),
        ],
        compiler_params=params(),
        name="second_conv",
    )(
        *scalars,
        second_parts,
        above,
        below,
        column_weights(second_weight),
        second_bias,
        hidden,
    )
    return out[None]


def solution(mesh):
    in_specs = (P("tm", None, None, None, "video", None),) + (P(),) * 11
    out_specs = P("tm", None, "video", None, None)
    return jax.shard_map(
        on_device, mesh=mesh, in_specs=in_specs, out_specs=out_specs, check_vma=False
    )
```

time: 332 us -> 149 us (0.45); the launches traced: 326 us -> 148 us
  matrix products: 144 us -> 1.51 us
  Pallas kernels: 0 us -> 96.4 us
  waiting for transfers between devices: 82.5 us -> 5.78 us
  local copies, waits for them, and re-layouts: 56.5 us -> 17.5 us
  starting transfers between devices: 34.6 us -> 23.2 us
  other arithmetic: 7.82 us -> 3.72 us
    dot_general x27 -> x1, matrix products: 144 us -> 1.51 us  [on_device(): lax.dot_general(got.reshape(source.size, 3 * 384), lanes, (((0,), (0,)),...]
    pallas_call x0 -> x6, Pallas kernels: none -> 96.4 us  [the longest x1 43.4 us: on_device(): pl.pallas_call(first_kernel, grid=(4,), in_specs=[*[SMEM] * 4, by_step((1...]
    ppermute x9 -> x4, waiting for transfers between devices: 75.3 us -> 5.77 us  [the longest x2 4.58 us: from_behind(): return lax.ppermute(value, axis, [(i, i + by) for i in range(devices - by)])]
    slice x13 -> x0, local copies, waits for them, and re-layouts: 48.1 us -> none  [the longest x8 47.6 us: convolve(): window[:, :, :, step_x:step_x + col_count]]
    unnamed x65 -> x19, local copies, waits for them, and re-layouts: 3.49 us -> 15.9 us
    ppermute x9 -> x4, starting transfers between devices: 26.2 us -> 14.8 us  [the longest x2 8.87 us: neighbour_bands(): return lax.ppermute(value, axis, pairs)]
    all_to_all x1, waiting for transfers between devices: 7.27 us -> 0.01 us  [on_device(): got = lax.all_to_all(sent, 'video', 0, 0, tiled=True)]
    convert_element_type x11 -> x1, other arithmetic: 6.29 us -> 0.68 us  [on_device(): live[:, None, None, None, None].astype(BF16)]
  transfers between devices with their start and end apart: 10 -> 5, of which waited for: 8 -> 3; matrix products, arithmetic and copies ran while one was open for 0% -> 1% of each run, Pallas kernels for 0% -> 5%
where the time goes in v1:
time: 149 us; the launch traced here: 148 us
  Pallas kernels  96.4 us (65%)
  starting transfers between devices  23.2 us (16%)
  local copies, waits for them, and re-layouts  17.5 us (12%)
  waiting for transfers between devices  5.78 us (4%)
  other arithmetic  3.72 us (2%)
  matrix products  1.51 us (1%)
    pallas_call x1, Pallas kernels, on_device(): pl.pallas_call(first_kernel, grid=(4,), in_specs=[*[SMEM] * 4, by_step((1...  43.4 us
    pallas_call x1, Pallas kernels, on_device(): pl.pallas_call(second_kernel, grid=(4,), in_specs=[*[SMEM] * 4, by_step((...  26.9 us
    pallas_call x1, Pallas kernels, on_device(): pl.pallas_call(input_kernel, grid=(rows5_n,), in_specs=[*[SMEM] * 4, whol...  17.3 us
    unnamed x19, local copies, waits for them, and re-layouts  15.9 us
    ppermute x2, starting transfers between devices, neighbour_bands(): return lax.ppermute(value, axis, pairs)  8.87 us
    all_to_all x1, starting transfers between devices, on_device(): got = lax.all_to_all(sent, 'video', 0, 0, tiled=True)  8.34 us
    pallas_call x2, Pallas kernels, column_weights(): pl.pallas_call(weight_kernel, grid=(a * b,), in_specs=[pl.BlockSpec((1, d...  6.78 us
    ppermute x2, starting transfers between devices, from_behind(): return lax.ppermute(value, axis, [(i, i + by) for i in range(devices - by)])  5.95 us
  transfers between devices with their start and end apart: 5, of which 3 were waited for; matrix products, arithmetic and copies ran while one was open for 1% of the time, Pallas kernels for 5%

profile of v1, /device:TPU:2, one launch (start us, length us, event | category | flops | bytes accessed | tf_op | source)
XLA Modules:
  0.0 148.2 jit_solution(3396848351699166888)
XLA Ops:
  0.0 0.7 and_convert_fusion
  0.7 1.4 fusion.4
  2.1 0.5 copy.16
  2.6 0.0 copy-start.4
  2.6 0.6 pad.6.clone
  3.2 1.0 reshape.20.own_ref
  4.2 4.0 %collective-permute-start = (bf16[64,768]{1,0:T(8,128)(2,1)S(1)}, bf16[64,768]{1,0:T(8,128)(2,1)S(1)}, u32[]{:S(2)}, u32[]{:S(2)}) collective-permute-start(bf16[64,768]{1,0:T(8,128)(2,1)S(1)} %reshape.20.own_ref), channel_id=1, source_target_pairs={{0,64},{32,96},{1,65},{33,97},{2,66},{34,98},{3,67},{35,99},{4,68}... | collective-permute-start | bytes 294920 | tf_op jit(solution)/shard_map/ppermute | solution.py:19
  8.2 1.9 %collective-permute-start.1 = (bf16[64,768]{1,0:T(8,128)(2,1)S(1)}, bf16[64,768]{1,0:T(8,128)(2,1)S(1)}, u32[]{:S(2)}, u32[]{:S(2)}) collective-permute-start(bf16[64,768]{1,0:T(8,128)(2,1)S(1)} %reshape.20.own_ref), channel_id=1, source_target_pairs={{0,32},{32,64},{64,96},{1,33},{33,65},{65,97},{2,34},{34,66},{66,9... | collective-permute-start | bytes 294920 | tf_op jit(solution)/shard_map/ppermute | solution.py:19
  10.2 0.3 collective-permute-done.far_ref
  10.4 4.3 %collective-permute-done.1.near_ref = bf16[64,768]{1,0:T(8,128)(2,1)S(1)} collective-permute-done((bf16[64,768]{1,0:T(8,128)(2,1)S(1)}, bf16[64,768]{1,0:T(8,128)(2,1)S(1)}, u32[]{:S(2)}, u32[]{:S(2)}) %collective-permute-start.1) | collective-permute-done | bytes 98336 | tf_op jit(solution)/shard_map/ppermute | solution.py:19
  14.7 0.0 copy-done.4
  14.7 2.1 %route.1 = bf16[256,1152]{1,0:T(8,128)(2,1)} custom-call(s32[16]{0:T(128)S(1)} %copy-done.4, bf16[64,768]{1,0:T(8,128)(2,1)S(1)} %collective-permute-done.far_ref, bf16[64,768]{1,0:T(8,128)(2,1)S(1)} %collective-permute-done.1.near_ref, bf16[64,768]{1,0:T(8,128)(2,1)S(1)} %reshape.20.own_ref), custom_call_target="tpu_custom_call" | custom-call | tf_op jit(solution)/shard_map/route/pallas_call | solution.py:351
  16.8 8.3 %all-to-all-start = ((bf16[32,8,1152]{2,1,0:T(8,128)(2,1)}), bf16[32,8,1152]{2,1,0:T(8,128)(2,1)S(1)}, u32[]{:S(2)}, u32[]{:S(2)}) async-start(bf16[32,8,1152]{2,1,0:T(8,128)(2,1)} %bitcast.4), calls=%async_computation | async-start | bytes 1179648 | tf_op jit(solution)/shard_map/all_to_all | solution.py:360
  25.2 0.0 copy-start.2
  25.2 3.3 %copy-done.2 = bf16[3,3,1152,384]{3,2,1,0:T(8,128)(2,1)S(1)} copy-done((bf16[3,3,1152,384]{3,2,1,0:T(8,128)(2,1)S(1)}, bf16[3,3,1152,384]{3,2,1,0:T(8,128)(2,1)}, u32[]{:S(2)}) %copy-start.2) | copy-done | bytes 7962648
  28.4 0.0 copy-start.7
  28.4 0.0 copy-start.8
  28.4 3.4 %column_weights.2.weight_ref = bf16[4,9,384,384]{3,2,1,0:T(8,128)(2,1)S(1)} custom-call(bf16[9,1152,384]{2,1,0:T(8,128)(2,1)S(1)} %bitcast.17), custom_call_target="tpu_custom_call" | custom-call | bytes 18579456 | tf_op jit(solution)/shard_map/column_weights/pallas_call | solution.py:88
  31.8 0.0 copy-start.1
  31.8 3.9 %copy-done.1 = bf16[4,9,384,384]{3,2,1,0:T(8,128)(2,1)} copy-done((bf16[4,9,384,384]{3,2,1,0:T(8,128)(2,1)}, bf16[4,9,384,384]{3,2,1,0:T(8,128)(2,1)S(1)}, u32[]{:S(2)}) %copy-start.1) | copy-done | bytes 10616856
  35.7 0.6 pad_add_fusion.place_ref
  36.3 0.0 copy-done.7
  36.3 1.1 fusion.2
  37.4 0.0 all-to-all-done
  37.4 0.0 copy-done.8
  37.4 1.5 %convolution_convert_fusion.planes_ref = bf16[1152,512]{1,0:T(8,128)(2,1)} fusion(bf16[256,512]{1,0:T(8,128)(2,1)S(1)} %copy-done.8, bf16[32,8,1152]{2,1,0:T(8,128)(2,1)S(1)} %all-to-all-done), kind=kOutput, calls=%fused_computation | convolution fusion | flops 302579712 | bytes 2031616 | tf_op jit(solution)/shard_map/dot_general | solution.py:371
  38.9 17.3 %input_conv.1 = (bf16[4,5,896,384]{3,2,1,0:T(8,128)(2,1)}, bf16[3,3,2,128,384]{4,3,2,1,0:T(8,128)(2,1)}) custom-call(s32[2]{0:T(128)} %pad_add_fusion.place_ref, s32[16]{0:T(128)} %routing_ref.7, s32[16]{0:T(128)} %counts_ref.5, s32[16]{0:T(128)} %offsets_ref.5, bf16[1152,512]{1,0:T(8,128)(2,1)} %convolution_convert_fusion.planes_ref, ...), custom_call_target="tpu_custom_call" | custom-call | tf_op jit(solution)/shard_map/input_conv/pallas_call | solution.py:394
  56.1 43.4 %first_conv.1 = (bf16[5,2,128,384]{3,2,1,0:T(8,128)(2,1)}, bf16[5,2,128,384]{3,2,1,0:T(8,128)(2,1)}, bf16[4,3,640,384]{3,2,1,0:T(8,128)(2,1)}) custom-call(s32[2]{0:T(128)} %pad_add_fusion.place_ref, s32[16]{0:T(128)} %routing_ref.7, s32[16]{0:T(128)} %counts_ref.5, s32[16]{0:T(128)} %offsets_ref.5, bf16[4,5,896,384]{3,2,1,0:T(8,128)(2,1)} %get-tuple-element.10.parts_ref, ...), custom_call_target="tpu_custom_call" | custom-call | tf_op jit(solution)/shard_map/first_conv/pallas_call | solution.py:419
  99.5 2.2 %collective-permute-start.2 = (bf16[5,2,128,384]{3,2,1,0:T(8,128)(2,1)}, bf16[5,2,128,384]{3,2,1,0:T(8,128)(2,1)S(1)}, u32[]{:S(2)}, u32[]{:S(2)}) collective-permute-start(bf16[5,2,128,384]{3,2,1,0:T(8,128)(2,1)} %get-tuple-element.12), channel_id=1, source_target_pairs={{0,1},{2,3},{3,4},{4,5},{6,7},{7,8},{8,9},{10,11},{11,12},{12,13},... | collective-permute-start | bytes 2949128 | tf_op jit(solution)/shard_map/ppermute | solution.py:31
  101.7 6.6 %collective-permute-start.3 = (bf16[5,2,128,384]{3,2,1,0:T(8,128)(2,1)}, bf16[5,2,128,384]{3,2,1,0:T(8,128)(2,1)S(1)}, u32[]{:S(2)}, u32[]{:S(2)}) collective-permute-start(bf16[5,2,128,384]{3,2,1,0:T(8,128)(2,1)} %get-tuple-element.13), channel_id=1, source_target_pairs={{0,31},{1,0},{3,2},{4,3},{5,4},{7,6},{8,7},{9,8},{11,10},{12,11},{... | collective-permute-start | bytes 2949128 | tf_op jit(solution)/shard_map/ppermute | solution.py:31
  108.4 0.0 copy-start.3
  108.4 3.3 %copy-done.3 = bf16[3,3,1152,384]{3,2,1,0:T(8,128)(2,1)S(1)} copy-done((bf16[3,3,1152,384]{3,2,1,0:T(8,128)(2,1)S(1)}, bf16[3,3,1152,384]{3,2,1,0:T(8,128)(2,1)}, u32[]{:S(2)}) %copy-start.3) | copy-done | bytes 7962648
  111.7 3.4 %column_weights.3.weight_ref = bf16[4,9,384,384]{3,2,1,0:T(8,128)(2,1)S(1)} custom-call(bf16[9,1152,384]{2,1,0:T(8,128)(2,1)S(1)} %bitcast.18), custom_call_target="tpu_custom_call" | custom-call | bytes 18579456 | tf_op jit(solution)/shard_map/column_weights/pallas_call | solution.py:88
  115.1 0.0 copy-start
  115.1 4.0 %copy-done = bf16[4,9,384,384]{3,2,1,0:T(8,128)(2,1)} copy-done((bf16[4,9,384,384]{3,2,1,0:T(8,128)(2,1)}, bf16[4,9,384,384]{3,2,1,0:T(8,128)(2,1)S(1)}, u32[]{:S(2)}) %copy-start) | copy-done | bytes 10616856
  119.1 0.0 collective-permute-done.2.above_ref
  119.1 0.0 copy-start.5
  119.1 1.2 collective-permute-done.3.below_ref
  120.3 0.0 copy-start.6
  120.3 0.0 copy-done.5
  120.3 1.0 copy-done.6
  121.3 26.9 %second_conv.1 = bf16[3,6,128,384]{3,2,1,0:T(8,128)(2,1)} custom-call(s32[2]{0:T(128)} %pad_add_fusion.place_ref, s32[16]{0:T(128)} %routing_ref.7, s32[16]{0:T(128)} %counts_ref.5, s32[16]{0:T(128)} %offsets_ref.5, bf16[4,3,640,384]{3,2,1,0:T(8,128)(2,1)} %get-tuple-element.11.parts_ref, bf16[5,2,128,384]{3,2,1,0:T(8,128)(2,1)} %copy-done.5, ...), custom_call_target="tpu_custom_call" | custom-call | tf_op jit(solution)/shard_map/second_conv/pallas_call | solution.py:447
Async XLA Ops:
  2.6 12.1 %copy-start.4 = (s32[16]{0:T(128)S(1)}, s32[16]{0:T(128)}, u32[]{:S(2)}) copy-start(s32[16]{0:T(128)} %routing_ref.7) | copy-start | bytes 196
  4.2 6.2 %collective-permute-start = (bf16[64,768]{1,0:T(8,128)(2,1)S(1)}, bf16[64,768]{1,0:T(8,128)(2,1)S(1)}, u32[]{:S(2)}, u32[]{:S(2)}) collective-permute-start(bf16[64,768]{1,0:T(8,128)(2,1)S(1)} %reshape.20.own_ref), channel_id=1, source_target_pairs={{0,64},{32,96},{1,65},{33,97},{2,66},{34,98},{3,67},{35,99},{4,68}... | collective-permute-start | bytes 294920 | tf_op jit(solution)/shard_map/ppermute | solution.py:19
  8.2 6.5 %collective-permute-start.1 = (bf16[64,768]{1,0:T(8,128)(2,1)S(1)}, bf16[64,768]{1,0:T(8,128)(2,1)S(1)}, u32[]{:S(2)}, u32[]{:S(2)}) collective-permute-start(bf16[64,768]{1,0:T(8,128)(2,1)S(1)} %reshape.20.own_ref), channel_id=1, source_target_pairs={{0,32},{32,64},{64,96},{1,33},{33,65},{65,97},{2,34},{34,66},{66,9... | collective-permute-start | bytes 294920 | tf_op jit(solution)/shard_map/ppermute | solution.py:19
  16.8 20.6 %all-to-all-start = ((bf16[32,8,1152]{2,1,0:T(8,128)(2,1)}), bf16[32,8,1152]{2,1,0:T(8,128)(2,1)S(1)}, u32[]{:S(2)}, u32[]{:S(2)}) async-start(bf16[32,8,1152]{2,1,0:T(8,128)(2,1)} %bitcast.4), calls=%async_computation | async-start | bytes 1179648 | tf_op jit(solution)/shard_map/all_to_all | solution.py:360
  25.2 3.3 %copy-start.2 = (bf16[3,3,1152,384]{3,2,1,0:T(8,128)(2,1)S(1)}, bf16[3,3,1152,384]{3,2,1,0:T(8,128)(2,1)}, u32[]{:S(2)}) copy-start(bf16[3,3,1152,384]{3,2,1,0:T(8,128)(2,1)} %param.20) | copy-start | bytes 23887876
  28.4 7.8 %copy-start.7 = (bf16[3,3,48,384]{3,2,1,0:T(8,128)(2,1)S(1)}, bf16[3,3,48,384]{3,2,1,0:T(8,128)(2,1)}, u32[]{:S(2)}) copy-start(bf16[3,3,48,384]{3,2,1,0:T(8,128)(2,1)} %param.17) | copy-start | bytes 995332
  28.4 9.0 %copy-start.8 = (bf16[256,512]{1,0:T(8,128)(2,1)S(1)}, bf16[256,512]{1,0:T(8,128)(2,1)}, u32[]{:S(2)}) copy-start(bf16[256,512]{1,0:T(8,128)(2,1)} %constant.30.clone) | copy-start | bytes 786436
  31.8 3.9 %copy-start.1 = (bf16[4,9,384,384]{3,2,1,0:T(8,128)(2,1)}, bf16[4,9,384,384]{3,2,1,0:T(8,128)(2,1)S(1)}, u32[]{:S(2)}) copy-start(bf16[4,9,384,384]{3,2,1,0:T(8,128)(2,1)S(1)} %column_weights.2.weight_ref) | copy-start | bytes 31850500
  99.5 19.6 %collective-permute-start.2 = (bf16[5,2,128,384]{3,2,1,0:T(8,128)(2,1)}, bf16[5,2,128,384]{3,2,1,0:T(8,128)(2,1)S(1)}, u32[]{:S(2)}, u32[]{:S(2)}) collective-permute-start(bf16[5,2,128,384]{3,2,1,0:T(8,128)(2,1)} %get-tuple-element.12), channel_id=1, source_target_pairs={{0,1},{2,3},{3,4},{4,5},{6,7},{7,8},{8,9},{10,11},{11,12},{12,13},... | collective-permute-start | bytes 2949128 | tf_op jit(solution)/shard_map/ppermute | solution.py:31
  101.7 18.6 %collective-permute-start.3 = (bf16[5,2,128,384]{3,2,1,0:T(8,128)(2,1)}, bf16[5,2,128,384]{3,2,1,0:T(8,128)(2,1)S(1)}, u32[]{:S(2)}, u32[]{:S(2)}) collective-permute-start(bf16[5,2,128,384]{3,2,1,0:T(8,128)(2,1)} %get-tuple-element.13), channel_id=1, source_target_pairs={{0,31},{1,0},{3,2},{4,3},{5,4},{7,6},{8,7},{9,8},{11,10},{12,11},{... | collective-permute-start | bytes 2949128 | tf_op jit(solution)/shard_map/ppermute | solution.py:31
  108.4 3.3 %copy-start.3 = (bf16[3,3,1152,384]{3,2,1,0:T(8,128)(2,1)S(1)}, bf16[3,3,1152,384]{3,2,1,0:T(8,128)(2,1)}, u32[]{:S(2)}) copy-start(bf16[3,3,1152,384]{3,2,1,0:T(8,128)(2,1)} %param.23) | copy-start | bytes 23887876
  115.1 4.0 %copy-start = (bf16[4,9,384,384]{3,2,1,0:T(8,128)(2,1)}, bf16[4,9,384,384]{3,2,1,0:T(8,128)(2,1)S(1)}, u32[]{:S(2)}) copy-start(bf16[4,9,384,384]{3,2,1,0:T(8,128)(2,1)S(1)} %column_weights.3.weight_ref) | copy-start | bytes 31850500
  119.1 1.2 copy-start.5
  120.3 1.0 copy-start.6

commit v2 on v1

v2 whole, which is shorter than its diff:
```python
import jax
import jax.numpy as jnp
import ml_dtypes
import numpy as np
from jax import lax
from jax.experimental import pallas as pl
from jax.experimental.pallas import tpu as pltpu
from jax.sharding import PartitionSpec as P

BANDS = 4
VPG = 2
F32 = jnp.float32
BF16 = jnp.bfloat16
VMEM_LIMIT = 60 << 20


def neighbour_bands(value, axis, down):
    count = lax.axis_size(axis)
    pairs = []
    for device in range(count):
        band = ((device + BANDS // 2) % count) % BANDS
        if down and band < BANDS - 1:
            pairs.append((device, (device + 1) % count))
        if not down and band > 0:
            pairs.append((device, (device - 1) % count))
    return lax.ppermute(value, axis, pairs)


def act(values, gain):
    scale = lax.rsqrt(jnp.mean(values * values, axis=-1, keepdims=True) + 1e-06)
    half = values * scale * (0.5 * gain)
    return half * (1.0 + jnp.tanh(half))


def column_parts(even, odd):
    rows = even.shape[0]
    pair = lax.broadcasted_iota(jnp.int32, (rows, 1), 0) % 64
    odd_before = jnp.where(pair == 0, 0.0, pltpu.roll(odd, 1, 0))
    even_after = jnp.where(pair == 63, 0.0, pltpu.roll(even, rows - 1, 0))
    return odd_before - odd, even + odd, odd - even, even - even_after


def route_kernel(place_ref, routing_ref, counts_ref, offsets_ref, own_ref, sent_ref):
    span_count, rows = sent_ref.shape[:2]
    lanes = own_ref.shape[0]
    span = place_ref[1]
    lane = lax.broadcasted_iota(jnp.int32, (1, lanes), 1)
    slot_of_lane = jnp.full((1, lanes), -1, jnp.int32)
    for v in range(routing_ref.shape[0]):
        live = (span >= offsets_ref[v]) & (span < offsets_ref[v] + counts_ref[v])
        slot = jnp.where(live, routing_ref[v], -1)
        slot_of_lane = jnp.where(lane // 4 == v, slot, slot_of_lane)
    row = lax.broadcasted_iota(jnp.int32, (rows, 1), 0)
    placed = (row // 8 + BANDS // 2) % (rows // 8)
    slot_of_row = (placed // BANDS) * VPG + (row // 4) % VPG
    pick = (slot_of_row == slot_of_lane) & (row % 4 == lane % 4)
    pick = jnp.where(pick, 1.0, 0.0).astype(BF16)
    moved = jnp.dot(pick, own_ref[...], preferred_element_type=F32)
    edge = jnp.zeros((rows, 96), F32)
    moved = jnp.concatenate([edge, moved, edge], axis=1)
    tail = jnp.zeros((8, 48), F32)
    reach = [jnp.where((k >= span) & (k <= span + 2), 1.0, 0.0) for k in range(span_count)]
    for pair in range(rows // 16):
        parts = []
        for device in (2 * pair, 2 * pair + 1):
            start = ((device + BANDS // 2) % BANDS) * 144
            window = moved[device * 8 : device * 8 + 8, start : start + 336]
            parts.append(jnp.concatenate([window, tail], axis=1))
        block = jnp.concatenate(parts, axis=0)
        for k in range(span_count):
            sent_ref[k, pair * 16 : pair * 16 + 16, :] = (block * reach[k]).astype(BF16)


def weight_copies(weight_ref, taps_ref, middle_ref, sems, which):
    depth = middle_ref.shape[0] // 3
    target = {0: taps_ref.at[0], 1: middle_ref, 2: taps_ref.at[3]}[which]
    return [
        pltpu.make_async_copy(
            weight_ref.at[3 * a + b, which * depth : (which + 1) * depth, :],
            target.at[a * depth : (a + 1) * depth, b * depth : (b + 1) * depth],
            sems.at[which, 3 * a + b],
        )
        for a in range(3)
        for b in range(3)
    ]


def mix_weights(taps_ref, middle_ref):
    size = 128

    def one_part(t, carry):
        at = pl.ds(pl.multiple_of(t * size, size), size)
        ends = 0.5 * (taps_ref[0, at].astype(F32) + taps_ref[3, at].astype(F32))
        middle = 0.5 * middle_ref[at].astype(F32)
        taps_ref[1, at] = (ends + middle).astype(BF16)
        taps_ref[2, at] = (ends - middle).astype(BF16)
        return carry

    lax.fori_loop(0, middle_ref.shape[0] // size, one_part, 0)


def video_spans(place_ref, routing_ref, counts_ref, offsets_ref):
    found = []
    for p in range(VPG):
        slot = (place_ref[0] // BANDS) * VPG + p
        first = jnp.int32(0)
        end = jnp.int32(0)
        for v in range(routing_ref.shape[0]):
            here = routing_ref[v] == slot
            first = jnp.where(here, offsets_ref[v], first)
            end = jnp.where(here, offsets_ref[v] + counts_ref[v], end)
        found.append((first, end))
    return found


def live_mask(spans, span, inside, rows):
    flags = [
        jnp.where((span >= first) & (span < end) & inside, 1.0, 0.0) for first, end in spans
    ]
    row = lax.broadcasted_iota(jnp.int32, (rows, 1), 0)
    return jnp.where(row < rows // 2, flags[0], flags[1])


def add_products(terms_ref, step, row, written, load, taps_ref):
    out_rows, size, channels = terms_ref.shape[1:]
    taps = [b for b in range(3) if 0 <= row - b < out_rows]
    first, last = taps[0], taps[-1] + 1
    stacked = jnp.concatenate([load(a * 128, size) for a in range(3)], axis=1)
    both = jnp.dot(
        stacked,
        taps_ref[step, :, first * channels : last * channels],
        preferred_element_type=F32,
    )
    for b in taps:
        term = both[:, (b - first) * channels : (b - first + 1) * channels]
        if row - b in written:
            terms_ref[step, row - b] += term
        else:
            terms_ref[step, row - b] = term
        written.add(row - b)


def first_kernel(
    place_ref,
    routing_ref,
    counts_ref,
    offsets_ref,
    got_ref,
    lanes_ref,
    in_taps_ref,
    in_bias_ref,
    first_gain_ref,
    weight_ref,
    bias_ref,
    gain_ref,
    hidden_ref,
    top_ref,
    bottom_ref,
    second_ref,
    planes_ref,
    parts_ref,
    taps_ref,
    middle_ref,
    terms_ref,
    sems,
):
    copies = [weight_copies(weight_ref, taps_ref, middle_ref, sems, k) for k in range(3)]
    for column in copies:
        for copy in column:
            copy.start()
    spans = video_spans(place_ref, routing_ref, counts_ref, offsets_ref)
    span_count = got_ref.shape[0]
    for k in range(span_count):
        planes_ref[k * 384 : (k + 1) * 384, :] = lax.dot_general(
            got_ref[k], lanes_ref[...], (((0,), (0,)), ((), ())), preferred_element_type=F32
        ).astype(BF16)
    in_bias = in_bias_ref[...]
    first_gain = first_gain_ref[...]
    in_rows = parts_ref.shape[1]
    frames = parts_ref.shape[2] // 128
    out_rows, size = terms_ref.shape[1:3]

    def input_row(row, carry):
        window_row = (place_ref[0] % BANDS) * out_rows - 1 + row
        inside = (window_row >= 0) & (window_row < out_rows * BANDS)
        own = jnp.clip(row - 1, 0, out_rows - 1)
        for f in range(frames):
            taps = []
            for a in range(3):
                s, k = divmod(f + a, 3)
                base = ((place_ref[1] + span_count - 2 + s) % span_count) * 384
                for b in range(3):
                    start = pl.multiple_of(base + k * 16 + (row + b) * 48, 16)
                    tap = planes_ref[pl.ds(start, 16), :]
                    taps += [tap[:, p * 128 : (p + 1) * 128] for p in range(4)]
            patch = jnp.concatenate(taps, axis=0)
            both = lax.dot_general(
                patch, in_taps_ref[...], (((0,), (0,)), ((), ())), preferred_element_type=F32
            )
            span = place_ref[1] + (f + 2) // 3 - 2
            mask = live_mask(spans, span, inside, 128)
            sides = []
            for side in range(2):
                values = both[:, side * 384 : (side + 1) * 384] + in_bias
                hidden = (values * mask).astype(BF16)
                if f >= frames - 3:

                    @pl.when(row <= out_rows)
                    def _(hidden=hidden, f=f, side=side):
                        hidden_ref[own, f - (frames - 3), side] = hidden

                sides.append(act(hidden.astype(F32), first_gain))
            for i, part in enumerate(column_parts(*sides)):
                parts_ref[i, row, f * 128 : (f + 1) * 128, :] = part.astype(BF16)
        return carry

    lax.fori_loop(0, in_rows, input_row, 0)

    for column in copies:
        for copy in column:
            copy.wait()
    mix_weights(taps_ref, middle_ref)

    def one_step(step, carry):
        written = set()
        for row in range(in_rows):
            add_products(
                terms_ref,
                step,
                row,
                written,
                lambda start, n, row=row: parts_ref[step, row, start : start + n, :],
                taps_ref,
            )
        return carry

    lax.fori_loop(0, 4, one_step, 0)

    bias = bias_ref[...]
    gain = gain_ref[...]
    for row in range(out_rows):

        def one_frame(f, carry, row=row):
            at = pl.ds(pl.multiple_of(f * 128, 128), 128)
            span = place_ref[1] + (f + 1) // 3 - 1
            mask = live_mask(spans, span, True, 128)
            mixed = terms_ref[1, row, at], terms_ref[2, row, at]
            even = terms_ref[0, row, at] + mixed[0] + mixed[1]
            odd = mixed[0] - mixed[1] - terms_ref[3, row, at]
            even = act((even + bias) * mask, gain)
            odd = act((odd + bias) * mask, gain)
            for edge_row, ref in ((0, top_ref), (out_rows - 1, bottom_ref)):
                if row == edge_row:
                    ref[f, 0] = even.astype(BF16)
                    ref[f, 1] = odd.astype(BF16)
            for i, part in enumerate(column_parts(even, odd)):
                second_ref[i, row, at, :] = part.astype(BF16)
            return carry

        lax.fori_loop(0, size // 128, one_frame, 0)


def write_line(line_ref, even, odd):
    for lane in range(3):
        cut = slice(lane * 128, lane * 128 + 128)
        line_ref[lane, pl.ds(0, 64, stride=2), :] = even[:, cut]
        line_ref[lane, pl.ds(1, 64, stride=2), :] = odd[:, cut]
    return jnp.concatenate([line_ref[lane] for lane in range(3)], axis=1).astype(BF16)


def video_lives(place_ref, routing_ref, counts_ref, offsets_ref):
    spans = video_spans(place_ref, routing_ref, counts_ref, offsets_ref)
    return [
        jnp.where((place_ref[1] >= first) & (place_ref[1] < end), 1.0, 0.0) for first, end in spans
    ]


def inner_kernel(
    place_ref,
    routing_ref,
    counts_ref,
    offsets_ref,
    second_ref,
    weight_ref,
    bias_ref,
    hidden_ref,
    out_ref,
    sums_ref,
    edge_taps_ref,
    parts_ref,
    taps_ref,
    middle_ref,
    terms_ref,
    line_ref,
    sems,
    part_sems,
    edge_sems,
):
    out_rows, size, channels = terms_ref.shape[1:]
    copies = [weight_copies(weight_ref, taps_ref, middle_ref, sems, k) for k in range(3)]
    parts = [
        pltpu.make_async_copy(second_ref.at[i], parts_ref.at[i], part_sems.at[i])
        for i in range(4)
    ]
    for k, i in ((0, 0), (2, 3), (1, 1)):
        parts[i].start()
        for copy in copies[k]:
            copy.start()
    parts[2].start()

    def one_step(step):
        written = set()
        for row in range(1, out_rows + 1):
            add_products(
                terms_ref,
                step,
                row,
                written,
                lambda start, n, row=row: parts_ref[step, row - 1, start : start + n, :],
                taps_ref,
            )

    for k, i in ((0, 0), (2, 3)):
        parts[i].wait()
        for copy in copies[k]:
            copy.wait()

    def end_steps(n, carry):
        one_step(n * 3)
        return carry

    def middle_steps(n, carry):
        one_step(n + 1)
        return carry

    lax.fori_loop(0, 2, end_steps, 0)
    for copy in copies[1]:
        copy.wait()
    parts[1].wait()
    parts[2].wait()
    mix_weights(taps_ref, middle_ref)
    edge_copies = [
        pltpu.make_async_copy(
            taps_ref.at[:, :, 2 * side * channels : (2 * side + 1) * channels],
            edge_taps_ref.at[side],
            edge_sems.at[side],
        )
        for side in range(2)
    ]
    for copy in edge_copies:
        copy.start()
    lax.fori_loop(0, 2, middle_steps, 0)

    bias = bias_ref[...]
    lives = video_lives(place_ref, routing_ref, counts_ref, offsets_ref)
    for row in range(out_rows):
        side = {0: 0, out_rows - 1: 1}.get(row)

        def one_frame(f, carry, row=row, side=side):
            for video in range(2):
                at = pl.ds(pl.multiple_of(f * 128 + video * 64, 64), 64)
                here = slice(video * 64, video * 64 + 64)
                mixed = terms_ref[1, row, at], terms_ref[2, row, at]
                even = terms_ref[0, row, at] + mixed[0] + mixed[1]
                odd = mixed[0] - mixed[1] - terms_ref[3, row, at]
                even = (even + bias + hidden_ref[row, f, 0, here].astype(F32)) * lives[video]
                odd = (odd + bias + hidden_ref[row, f, 1, here].astype(F32)) * lives[video]
                if side is None:
                    out_ref[f, video * out_rows + row] = write_line(line_ref, even, odd)
                else:
                    sums_ref[side, 0, at] = even
                    sums_ref[side, 1, at] = odd
            return carry

        lax.fori_loop(0, size // 128, one_frame, 0)
    for copy in edge_copies:
        copy.wait()


def outer_kernel(
    place_ref,
    routing_ref,
    counts_ref,
    offsets_ref,
    inner_ref,
    above_ref,
    below_ref,
    taps_ref,
    sums_ref,
    out_ref,
    halo_ref,
    terms_ref,
    line_ref,
    ready_ref,
    sems,
):
    step = pl.program_id(0)
    size = terms_ref.shape[2]
    rows_per_video = out_ref.shape[1] // VPG

    @pl.when(step == 0)
    def _():
        def one_frame(f, carry):
            at = pl.ds(pl.multiple_of(f * 128, 128), 128)
            for side, ref in enumerate((above_ref, below_ref)):
                even, odd = ref[f, 0].astype(F32), ref[f, 1].astype(F32)
                for i, part in enumerate(column_parts(even, odd)):
                    halo_ref[i, side, at, :] = part.astype(BF16)
            return carry

        lax.fori_loop(0, halo_ref.shape[2] // 128, one_frame, 0)

    for side in range(2):
        stacked = jnp.concatenate(
            [halo_ref[step, side, a * 128 : a * 128 + size, :] for a in range(3)], axis=1
        )
        terms_ref[step, side] = jnp.dot(stacked, taps_ref[side, 0], preferred_element_type=F32)

    @pl.when(step == 3)
    def _():
        lives = video_lives(place_ref, routing_ref, counts_ref, offsets_ref)
        copies = []
        for f in range(size // 128):
            for side in range(2):
                for video in range(VPG):
                    at = slice(f * 128 + video * 64, f * 128 + video * 64 + 64)
                    mixed = terms_ref[1, side, at], terms_ref[2, side, at]
                    even = terms_ref[0, side, at] + mixed[0] + mixed[1]
                    odd = mixed[0] - mixed[1] - terms_ref[3, side, at]
                    even = sums_ref[side, 0, at] + even * lives[video]
                    odd = sums_ref[side, 1, at] + odd * lives[video]
                    n = len(copies)
                    ready_ref[n] = write_line(line_ref, even, odd)
                    row = video * rows_per_video + side * (rows_per_video - 1)
                    copies.append(
                        pltpu.make_async_copy(ready_ref.at[n], out_ref.at[f, row], sems.at[n])
                    )
                    copies[-1].start()
        for copy in copies:
            copy.wait()


def whole(shape):
    return pl.BlockSpec(shape, lambda *_: (0,) * len(shape))


SMEM = pl.BlockSpec(memory_space=pltpu.SMEM)
VMEM = pl.BlockSpec(memory_space=pltpu.VMEM)
ANY = pl.BlockSpec(memory_space=pl.ANY)


def params():
    return pltpu.CompilerParams(vmem_limit_bytes=VMEM_LIMIT)


def on_device(
    latent,
    routing,
    counts,
    offsets,
    in_weight,
    in_bias,
    first_gain,
    first_weight,
    first_bias,
    second_gain,
    second_weight,
    second_bias,
):
    groups = lax.axis_size("video")
    spans = lax.axis_size("tm")
    _, span_frames, videos, window_rows, local_cols, zdim = latent.shape
    row_count = window_rows // BANDS
    channels = in_weight.shape[-1]
    pairs = groups * local_cols // 2
    span_index = lax.axis_index("tm")
    device_index = lax.axis_index("video")

    my_placed = (device_index + BANDS // 2) % groups
    place = jnp.stack([my_placed, span_index])
    scalars = (place, routing, counts, offsets)

    own = jnp.transpose(latent[0], (1, 3, 2, 0, 4))
    own = own.reshape(videos * local_cols, window_rows * span_frames * zdim)
    chunk = VPG * local_cols
    sent = pl.pallas_call(
        route_kernel,
        in_specs=[SMEM] * 4 + [VMEM],
        out_specs=VMEM,
        out_shape=jax.ShapeDtypeStruct((spans, groups * chunk, 384), BF16),
        compiler_params=pltpu.CompilerParams(vmem_limit_bytes=16 << 20),
        name="route",
    )(*scalars, own)
    sent = sent.reshape(spans * groups, chunk, 384)
    got = lax.all_to_all(sent, ("tm", "video"), 0, 0, tiled=True)
    got = got.reshape(spans, groups * chunk, 384)

    source = np.arange(groups * VPG * local_cols)
    source_col = (source // (VPG * local_cols)) * local_cols + source % local_cols
    source_video = (source // local_cols) % VPG
    pair = np.arange(pairs)
    wanted = np.stack([2 * pair - 1, 2 * pair, 2 * pair + 1, 2 * pair + 2])
    lanes = (source_col[:, None, None, None] == wanted[:, None, :]) & (
        source_video[:, None, None, None] == np.arange(VPG)[:, None]
    )
    lanes = lanes.reshape(source.size, 4 * VPG * pairs).astype(ml_dtypes.bfloat16)
    frames = 3 * span_frames
    in_frames, mid_frames = frames - 2, frames - 4
    width = VPG * pairs
    rows5_n = row_count + 2

    zero = jnp.zeros(in_weight.shape[:2] + (zdim, channels), BF16)
    in_taps = jnp.concatenate(
        [
            jnp.concatenate([in_weight, zero], axis=2),
            jnp.concatenate([zero, in_weight], axis=2),
        ],
        axis=3,
    ).reshape(-1, 2 * channels)

    depth = 3 * channels
    raw_shape = (9, depth, channels)
    edge_shape = (mid_frames, 2, width, channels)
    part_shape = (4, row_count, mid_frames * width, channels)
    hidden_shape = (row_count, span_frames, 2, width, channels)
    hidden, top, bottom, second_parts = pl.pallas_call(
        first_kernel,
        in_specs=[SMEM] * 4 + [VMEM] * 5 + [ANY] + [VMEM] * 2,
        out_specs=[VMEM] * 4,
        out_shape=[
            jax.ShapeDtypeStruct(shape, BF16)
            for shape in (hidden_shape, edge_shape, edge_shape, part_shape)
        ],
        scratch_shapes=[
            pltpu.VMEM((spans * 384, 4 * width), BF16),
            pltpu.VMEM((4, rows5_n, in_frames * width, channels), BF16),
            pltpu.VMEM((4, depth, depth), BF16),
            pltpu.VMEM((depth, depth), BF16),
            pltpu.VMEM((4, row_count, mid_frames * width, channels), F32),
            pltpu.SemaphoreType.DMA((3, 9)),
        ],
        compiler_params=params(),
        name="first_conv",
    )(
        *scalars,
        got,
        lanes,
        in_taps,
        in_bias,
        first_gain,
        first_weight.reshape(raw_shape),
        first_bias,
        second_gain,
    )

    above = neighbour_bands(bottom, "video", True)
    below = neighbour_bands(top, "video", False)

    out_shape = (span_frames, VPG * row_count, 2 * pairs, channels)
    sums_shape = (2, 2, span_frames * width, channels)
    inner, sums, edge_taps = pl.pallas_call(
        inner_kernel,
        in_specs=[SMEM] * 4 + [ANY, ANY, VMEM, VMEM],
        out_specs=[VMEM, VMEM, ANY],
        out_shape=[
            jax.ShapeDtypeStruct(out_shape, BF16),
            jax.ShapeDtypeStruct(sums_shape, F32),
            jax.ShapeDtypeStruct((2, 4, depth, channels), BF16),
        ],
        scratch_shapes=[
            pltpu.VMEM(part_shape, BF16),
            pltpu.VMEM((4, depth, depth), BF16),
            pltpu.VMEM((depth, depth), BF16),
            pltpu.VMEM((4, row_count, span_frames * width, channels), F32),
            pltpu.VMEM((3, 2 * pairs, 128), F32),
            pltpu.SemaphoreType.DMA((3, 9)),
            pltpu.SemaphoreType.DMA((4,)),
            pltpu.SemaphoreType.DMA((2,)),
        ],
        compiler_params=params(),
        cost_estimate=pl.CostEstimate(
            flops=12 * 10**9, bytes_accessed=24 * 10**6, transcendentals=0
        ),
        name="second_conv_inner",
    )(*scalars, second_parts, second_weight.reshape(raw_shape), second_bias, hidden)

    out = pl.pallas_call(
        outer_kernel,
        grid=(4,),
        in_specs=[
            *[SMEM] * 4,
            ANY,
            whole(edge_shape),
            whole(edge_shape),
            pl.BlockSpec((2, 1, depth, channels), lambda i: (0, i, 0, 0)),
            whole(sums_shape),
        ],
        out_specs=ANY,
        out_shape=jax.ShapeDtypeStruct(out_shape, BF16),
        input_output_aliases={4: 0},
        scratch_shapes=[
            pltpu.VMEM((4, 2, mid_frames * width, channels), BF16),
            pltpu.VMEM((4, 2, span_frames * width, channels), F32),
            pltpu.VMEM((3, 2 * pairs, 128), F32),
            pltpu.VMEM((span_frames * 2 * VPG, 2 * pairs, channels), BF16),
            pltpu.SemaphoreType.DMA((span_frames * 2 * VPG,)),
        ],
        compiler_params=params(),
        name="second_conv_outer",
    )(*scalars, inner, above, below, edge_taps, sums)
    return out[None]


def solution(mesh):
    in_specs = (P("tm", None, None, None, "video", None),) + (P(),) * 11
    out_specs = P("tm", None, "video", None, None)
    return jax.shard_map(
        on_device, mesh=mesh, in_specs=in_specs, out_specs=out_specs, check_vma=False
    )
```

time: 149 us -> 128 us (0.86)
  local copies, waits for them, and re-layouts: 17.5 us -> 4.33 us
  Pallas kernels: 96.4 us -> 85.7 us
  waiting for transfers between devices: 5.78 us -> 15.2 us
  starting transfers between devices: 23.2 us -> 19.6 us
  other arithmetic: 3.72 us -> 1.09 us
  matrix products: 1.51 us -> 0 us
    all_to_all x1, waiting for transfers between devices: 0.01 us -> 15.2 us  [on_device(): got = lax.all_to_all(sent, ('tm', 'video'), 0, 0, tiled=True)]
    unnamed x19 -> x16, local copies, waits for them, and re-layouts: 15.9 us -> 2.17 us
    pallas_call x6 -> x4, Pallas kernels: 96.4 us -> 85.7 us  [the longest x1 51.2 us: on_device(): pl.pallas_call(first_kernel, in_specs=[SMEM] * 4 + [VMEM] * 5 + [ANY] + [...]
    ppermute x2 -> x0, starting transfers between devices: 5.95 us -> none  [from_behind(): return lax.ppermute(value, axis, [(i, i + by) for i in range(devices - by)])]
    ppermute x2 -> x0, waiting for transfers between devices: 4.58 us -> none  [from_behind(): return lax.ppermute(value, axis, [(i, i + by) for i in range(devices - by)])]
    all_to_all x1, starting transfers between devices: 8.34 us -> 10.5 us  [on_device(): got = lax.all_to_all(sent, ('tm', 'video'), 0, 0, tiled=True)]
    transpose x0 -> x1, local copies, waits for them, and re-layouts: none -> 1.6 us  [on_device(): own = jnp.transpose(latent[0], (1, 3, 2, 0, 4))]
    dot_general x1 -> x0, matrix products: 1.51 us -> none  [on_device(): lax.dot_general(got.reshape(source.size, 3 * 384), lanes, (((0,), (0,)),...]
  transfers between devices with their start and end apart: 5 -> 3, of which waited for: 3 -> 1; matrix products, arithmetic and copies ran while one was open for 1% -> 1% of each run, Pallas kernels for 5% -> 18%
where the time goes in v2:
time: 128 us; the launch traced here: 126 us
  Pallas kernels  85.7 us (67%)
  starting transfers between devices  19.6 us (15%)
  waiting for transfers between devices  15.2 us (12%)
  local copies, waits for them, and re-layouts  4.33 us (3%)
    pallas_call x1, Pallas kernels, on_device(): pl.pallas_call(first_kernel, in_specs=[SMEM] * 4 + [VMEM] * 5 + [ANY] + [...  51.2 us
    pallas_call x1, Pallas kernels, on_device(): pl.pallas_call(inner_kernel, in_specs=[SMEM] * 4 + [ANY, ANY, VMEM, VMEM]...  22.4 us
    all_to_all x1, waiting for transfers between devices, on_device(): got = lax.all_to_all(sent, ('tm', 'video'), 0, 0, tiled=True)  15.2 us
    all_to_all x1, starting transfers between devices, on_device(): got = lax.all_to_all(sent, ('tm', 'video'), 0, 0, tiled=True)  10.5 us
    pallas_call x1, Pallas kernels, on_device(): pl.pallas_call(outer_kernel, grid=(4,), in_specs=[*[SMEM] * 4, ANY, whole...  10.1 us
    ppermute x2, starting transfers between devices, neighbour_bands(): return lax.ppermute(value, axis, pairs)  9.06 us
  transfers between devices with their start and end apart: 3, of which 1 were waited for; matrix products, arithmetic and copies ran while one was open for 1% of the time, Pallas kernels for 18%

profile of v2, /device:TPU:2, one launch (start us, length us, event | category | flops | bytes accessed | tf_op | source)
XLA Modules:
  0.0 126.2 jit_solution(11433673983941901017)
XLA Ops:
  0.0 0.0 copy-start.2
  0.0 0.0 copy-start.1
  0.0 0.0 copy-start
  0.0 1.6 %copy.16 = bf16[16,4,12,3,16]{4,3,2,1,0:T(4,128)(2,1)S(1)} copy(bf16[16,4,12,3,16]{4,1,2,0,3:T(4,128)(2,1)} %bitcast.14) | data formatting | bytes 147456 | tf_op jit(solution)/shard_map/transpose | solution.py:483
  1.6 0.0 copy-start.7
  1.6 0.6 reshape.18.own_ref
  2.2 0.1 pad_add_fusion.place_ref
  2.3 0.0 copy-done.2
  2.3 0.0 copy-done.1
  2.3 0.0 copy-done
  2.3 0.0 copy-start.3
  2.3 2.0 %route.1 = bf16[4,256,384]{2,1,0:T(8,128)(2,1)} custom-call(s32[2]{0:T(128)S(1)} %pad_add_fusion.place_ref, s32[16]{0:T(128)S(1)} %copy-done, s32[16]{0:T(128)S(1)} %copy-done.1, s32[16]{0:T(128)S(1)} %copy-done.2, bf16[64,576]{1,0:T(8,128)(2,1)S(1)} %reshape.18.own_ref), custom_call_target="tpu_custom_call" | custom-call | tf_op jit(solution)/shard_map/route/pallas_call | solution.py:486
  4.3 10.5 %all-to-all-start = ((bf16[128,8,384]{2,1,0:T(8,128)(2,1)}), bf16[128,8,384]{2,1,0:T(8,128)(2,1)S(1)}, u32[]{:S(2)}, u32[]{:S(2)}) async-start(bf16[128,8,384]{2,1,0:T(8,128)(2,1)} %bitcast.4), calls=%async_computation | async-start | bytes 1572864 | tf_op jit(solution)/shard_map/all_to_all | solution.py:495
  14.8 0.0 copy-done.7
  14.8 1.0 fusion.2
  15.8 0.0 copy-done.3
  15.8 15.2 %all-to-all-done = bf16[128,8,384]{2,1,0:T(8,128)(2,1)S(1)} async-done(((bf16[128,8,384]{2,1,0:T(8,128)(2,1)}), bf16[128,8,384]{2,1,0:T(8,128)(2,1)S(1)}, u32[]{:S(2)}, u32[]{:S(2)}) %all-to-all-start) | async-done | bytes 786464 | tf_op jit(solution)/shard_map/all_to_all | solution.py:495
  31.0 0.0 copy-start.4
  31.0 0.9 copy-done.4
  31.9 51.2 %first_conv.1 = (bf16[3,3,2,128,384]{4,3,2,1,0:T(8,128)(2,1)}, bf16[5,2,128,384]{3,2,1,0:T(8,128)(2,1)}, bf16[5,2,128,384]{3,2,1,0:T(8,128)(2,1)}, bf16[4,3,640,384]{3,2,1,0:T(8,128)(2,1)}) custom-call(s32[2]{0:T(128)} %copy-done.3, s32[16]{0:T(128)} %routing_ref.7, s32[16]{0:T(128)} %counts_ref.7, s32[16]{0:T(128)} %offsets_ref.7, ...), custom_call_target="tpu_custom_call" | custom-call | tf_op jit(solution)/shard_map/first_conv/pallas_call | solution.py:526
  83.1 1.9 %collective-permute-start = (bf16[5,2,128,384]{3,2,1,0:T(8,128)(2,1)}, bf16[5,2,128,384]{3,2,1,0:T(8,128)(2,1)S(1)}, u32[]{:S(2)}, u32[]{:S(2)}) collective-permute-start(bf16[5,2,128,384]{3,2,1,0:T(8,128)(2,1)} %get-tuple-element.15), channel_id=1, source_target_pairs={{0,1},{2,3},{3,4},{4,5},{6,7},{7,8},{8,9},{10,11},{11,12},{12,13},... | collective-permute-start | bytes 2949128 | tf_op jit(solution)/shard_map/ppermute | solution.py:26
  85.1 7.1 %collective-permute-start.1 = (bf16[5,2,128,384]{3,2,1,0:T(8,128)(2,1)}, bf16[5,2,128,384]{3,2,1,0:T(8,128)(2,1)S(1)}, u32[]{:S(2)}, u32[]{:S(2)}) collective-permute-start(bf16[5,2,128,384]{3,2,1,0:T(8,128)(2,1)} %get-tuple-element.16), channel_id=1, source_target_pairs={{0,31},{1,0},{3,2},{4,3},{5,4},{7,6},{8,7},{9,8},{11,10},{12,11},{... | collective-permute-start | bytes 2949128 | tf_op jit(solution)/shard_map/ppermute | solution.py:26
  92.2 22.4 %second_conv_inner.1 = (bf16[3,6,128,384]{3,2,1,0:T(8,128)(2,1)}, f32[2,2,384,384]{3,2,1,0:T(8,128)}, bf16[2,4,1152,384]{3,2,1,0:T(8,128)(2,1)}) custom-call(s32[2]{0:T(128)} %copy-done.3, s32[16]{0:T(128)} %routing_ref.7, s32[16]{0:T(128)} %counts_ref.7, s32[16]{0:T(128)} %offsets_ref.7, bf16[4,3,640,384]{3,2,1,0:T(8,128)(2,1)} %get-tuple-element.12.second_ref, ...), custom_call_target="tpu_custom_call" | custom-call | flops 12000000000 | bytes 24000000 | tf_op jit(solution)/shard_map/second_conv_inner/pallas_call | solution.py:561
  114.6 0.0 collective-permute-done.above_ref
  114.7 0.0 copy-start.5
  114.7 0.0 collective-permute-done.1.below_ref
  114.7 0.0 copy-start.6
  114.7 1.0 copy-done.5
  115.6 0.3 copy-done.6
  115.9 10.1 %second_conv_outer.1 = bf16[3,6,128,384]{3,2,1,0:T(8,128)(2,1)} custom-call(s32[2]{0:T(128)} %copy-done.3, s32[16]{0:T(128)} %routing_ref.7, s32[16]{0:T(128)} %counts_ref.7, s32[16]{0:T(128)} %offsets_ref.7, bf16[3,6,128,384]{3,2,1,0:T(8,128)(2,1)} %get-tuple-element.14.inner_ref, ...), custom_call_target="tpu_custom_call", output_to_operand_aliasing={{}: (4, {})} | custom-call | tf_op jit(solution)/shard_map/second_conv_outer/pallas_call | solution.py:587
Async XLA Ops:
  0.0 2.3 %copy-start.2 = (s32[16]{0:T(128)S(1)}, s32[16]{0:T(128)}, u32[]{:S(2)}) copy-start(s32[16]{0:T(128)} %offsets_ref.7) | copy-start | bytes 196
  0.0 2.3 %copy-start.1 = (s32[16]{0:T(128)S(1)}, s32[16]{0:T(128)}, u32[]{:S(2)}) copy-start(s32[16]{0:T(128)} %counts_ref.7) | copy-start | bytes 196
  0.0 2.3 %copy-start = (s32[16]{0:T(128)S(1)}, s32[16]{0:T(128)}, u32[]{:S(2)}) copy-start(s32[16]{0:T(128)} %routing_ref.7) | copy-start | bytes 196
  1.6 13.2 %copy-start.7 = (bf16[3,3,48,384]{3,2,1,0:T(8,128)(2,1)S(1)}, bf16[3,3,48,384]{3,2,1,0:T(8,128)(2,1)}, u32[]{:S(2)}) copy-start(bf16[3,3,48,384]{3,2,1,0:T(8,128)(2,1)} %param.17) | copy-start | bytes 995332
  2.3 13.5 %copy-start.3 = (s32[2]{0:T(128)}, s32[2]{0:T(128)S(1)}, u32[]{:S(2)}) copy-start(s32[2]{0:T(128)S(1)} %pad_add_fusion.place_ref) | copy-start | bytes 28
  4.3 26.7 %all-to-all-start = ((bf16[128,8,384]{2,1,0:T(8,128)(2,1)}), bf16[128,8,384]{2,1,0:T(8,128)(2,1)S(1)}, u32[]{:S(2)}, u32[]{:S(2)}) async-start(bf16[128,8,384]{2,1,0:T(8,128)(2,1)} %bitcast.4), calls=%async_computation | async-start | bytes 1572864 | tf_op jit(solution)/shard_map/all_to_all | solution.py:495
  31.0 0.9 copy-start.4
  83.1 31.5 %collective-permute-start = (bf16[5,2,128,384]{3,2,1,0:T(8,128)(2,1)}, bf16[5,2,128,384]{3,2,1,0:T(8,128)(2,1)S(1)}, u32[]{:S(2)}, u32[]{:S(2)}) collective-permute-start(bf16[5,2,128,384]{3,2,1,0:T(8,128)(2,1)} %get-tuple-element.15), channel_id=1, source_target_pairs={{0,1},{2,3},{3,4},{4,5},{6,7},{7,8},{8,9},{10,11},{11,12},{12,13},... | collective-permute-start | bytes 2949128 | tf_op jit(solution)/shard_map/ppermute | solution.py:26
  85.1 29.6 %collective-permute-start.1 = (bf16[5,2,128,384]{3,2,1,0:T(8,128)(2,1)}, bf16[5,2,128,384]{3,2,1,0:T(8,128)(2,1)S(1)}, u32[]{:S(2)}, u32[]{:S(2)}) collective-permute-start(bf16[5,2,128,384]{3,2,1,0:T(8,128)(2,1)} %get-tuple-element.16), channel_id=1, source_target_pairs={{0,31},{1,0},{3,2},{4,3},{5,4},{7,6},{8,7},{9,8},{11,10},{12,11},{... | collective-permute-start | bytes 2949128 | tf_op jit(solution)/shard_map/ppermute | solution.py:26
  114.7 1.0 copy-start.5
  114.7 1.2 copy-start.6
